TPU v7x, 256 devices: a whole 4x4x8 slice. The times are simulated.
256 devices in a mesh: dp: 8 (over z), expert: 32 (over y, x, core).
Axes of the slice: x: 4, y: 4, z: 8, core: 2. Of those that a mesh axis runs over, the one named last changes fastest.
Arguments:
- tokens: bfloat16 [40960, 2048], P(('dp', 'expert')), may hold values from -6 to 6
- expert_of: int32 [40960, 1], P(('dp', 'expert')), may hold values from 0 to 31; in each aligned block of 160 rows (0 to 159, 160 to 319, ...) at most 10 rows name the same one
- w_gate: bfloat16 [32, 2048, 768], P('expert'), may hold values from -0.125 to 0.125
- w_up: bfloat16 [32, 2048, 768], P('expert'), may hold values from -0.125 to 0.125
- w_down: bfloat16 [32, 768, 2048], P('expert'), may hold values from -0.21875 to 0.21875
- grad_out: bfloat16 [40960, 2048], P(('dp', 'expert')), may hold values from -6 to 6
Outputs:
- mixed: bfloat16 [40960, 2048], P(('dp', 'expert'))
- grad_tokens: bfloat16 [40960, 2048], P(('dp', 'expert'))
- grad_gate: bfloat16 [32, 2048, 768], P('expert', 'dp')
- grad_up: bfloat16 [32, 2048, 768], P('expert', 'dp')
- grad_down: bfloat16 [32, 768, 2048], P('expert', 'dp')
Inputs may be any that keep to these rules, and one draw needn't show every extreme that they name: `expert_of`: within the rows of one device (aligned blocks of 160 rows) no expert is named by more than 10 rows, and in every draw some block names some expert exactly 10 times.
All inputs are finite; a program needn't handle non-finite values.
Results may differ from a plain program's by a relative error of at most 0.005.
Values may be sent and summed in bfloat16 or wider, within the bound.
No kernel may reach another device: no remote copies, remote signals or barrier semaphores. Data moves between devices by JAX's collectives and lax.ppermute only.
A program may use at most 128 MiB of HBM per device.

v0:
```python
import jax
import jax.numpy as jnp
from jax import lax
from jax.sharding import PartitionSpec as P


def shards(tokens, expert_of, w_gate, w_up, w_down, grad_out):
    rows = tokens.shape[0]
    width = tokens.shape[1]
    peers = lax.axis_size("expert")
    groups = lax.axis_size("dp")
    slots = 2 * rows // peers
    gate_w = w_gate[0]
    up_w = w_up[0]
    down_w = w_down[0]
    hidden = gate_w.shape[1]
    scale = float(rows * groups) ** (-0.5)
    chosen = expert_of[:, 0]
    onehot = (chosen[:, None] == jnp.arange(peers, dtype=jnp.int32)[None, :]).astype(jnp.int32)
    ranks = jnp.sum((jnp.cumsum(onehot, axis=0) - 1) * onehot, axis=1)
    target = chosen * slots + ranks
    placing = (jnp.arange(peers * slots, dtype=jnp.int32)[:, None] == target[None, :]).astype(
        jnp.bfloat16
    )
    outgoing = jnp.dot(placing, tokens, preferred_element_type=jnp.float32).astype(jnp.bfloat16)
    outgoing = outgoing.reshape(peers, slots, width)
    send_grad = jnp.dot(placing, grad_out, preferred_element_type=jnp.float32).astype(jnp.bfloat16)
    send_grad = send_grad.reshape(peers, slots, width)
    arrived = lax.all_to_all(outgoing, "expert", split_axis=0, concat_axis=0, tiled=True)
    gate_part = jnp.einsum("pcd,df->pcf", arrived, gate_w, preferred_element_type=jnp.float32)
    up_part = jnp.einsum("pcd,df->pcf", arrived, up_w, preferred_element_type=jnp.float32)
    act_part = (jax.nn.silu(gate_part) * up_part).astype(jnp.bfloat16)
    result = jnp.einsum("pcf,fd->pcd", act_part, down_w, preferred_element_type=jnp.float32).astype(
        jnp.bfloat16
    )
    returned_part = lax.all_to_all(result, "expert", split_axis=0, concat_axis=0, tiled=True)
    returned = returned_part.reshape(peers * slots, width)
    received = arrived.reshape(peers * slots, width)
    gate_pre = gate_part.reshape(peers * slots, hidden)
    up_pre = up_part.reshape(peers * slots, hidden)
    swish = jax.nn.silu(gate_pre)
    act = (swish * up_pre).astype(jnp.bfloat16)
    arriving = lax.all_to_all(send_grad, "expert", split_axis=0, concat_axis=0, tiled=True)
    arriving = arriving.reshape(peers * slots, width)
    grad_act = jnp.einsum("sd,fd->sf", arriving, down_w, preferred_element_type=jnp.float32)
    sig = jax.nn.sigmoid(gate_pre)
    grad_gpre = (grad_act * up_pre * sig * (1.0 + gate_pre * (1.0 - sig))).astype(jnp.bfloat16)
    grad_upre = (grad_act * swish).astype(jnp.bfloat16)
    input_grad = jnp.einsum("sf,df->sd", grad_gpre, gate_w, preferred_element_type=jnp.float32)
    input_grad = (
        input_grad + jnp.einsum("sf,df->sd", grad_upre, up_w, preferred_element_type=jnp.float32)
    ).astype(jnp.bfloat16)
    back_grad = lax.all_to_all(
        input_grad.reshape(peers, slots, width), "expert", split_axis=0, concat_axis=0, tiled=True
    )
    back_grad = back_grad.reshape(peers * slots, width)
    mixed = jnp.einsum("st,sd->td", placing, returned, preferred_element_type=jnp.float32).astype(
        jnp.bfloat16
    )
    grad_tokens = jnp.einsum(
        "st,sd->td", placing, back_grad, preferred_element_type=jnp.float32
    ).astype(jnp.bfloat16)
    both_grads = jnp.concatenate([grad_gpre, grad_upre], axis=1)
    columns = received
    gate_up_sum = lax.psum_scatter(
        jnp.einsum("sr,sf->rf", columns, both_grads, preferred_element_type=jnp.float32),
        "dp",
        scatter_dimension=0,
        tiled=True,
    )
    columns = act
    down_sum = lax.psum_scatter(
        jnp.einsum("sr,sd->rd", columns, arriving, preferred_element_type=jnp.float32),
        "dp",
        scatter_dimension=0,
        tiled=True,
    )
    grad_gate = (gate_up_sum[:, :hidden] * scale).astype(jnp.bfloat16)[None]
    grad_up = (gate_up_sum[:, hidden:] * scale).astype(jnp.bfloat16)[None]
    grad_down = (down_sum * scale).astype(jnp.bfloat16)[None]
    return (mixed, grad_tokens, grad_gate, grad_up, grad_down)


def solution(mesh):
    in_specs = (
        P(("dp", "expert"), None),
        P(("dp", "expert"), None),
        P("expert", None, None),
        P("expert", None, None),
        P("expert", None, None),
        P(("dp", "expert"), None),
    )
    out_specs = (
        P(("dp", "expert"), None),
        P(("dp", "expert"), None),
        P("expert", "dp", None),
        P("expert", "dp", None),
        P("expert", "dp", None),
    )
    return jax.shard_map(shards, mesh=mesh, in_specs=in_specs, out_specs=out_specs, check_vma=False)
```

profile of v0, /device:TPU:2, one launch (start us, length us, event | category | flops | bytes accessed | tf_op | source)
XLA Modules:
  0.0 313.6 jit_solution(4928549274959021263)
XLA Ops:
  7.2 0.0 copy-start
  7.2 0.8 iota_compare_fusion.5
  8.0 0.6 reduce-window.6
  8.6 0.2 slice_reduce_fusion
  8.9 0.1 bitcast_bitcast_fusion
  8.9 0.7 fusion.38
  9.6 0.7 multiply_add_fusion
  10.3 2.7 convolution_convert_fusion.1
  13.0 3.3 %reshape.59 = bf16[32,10,2048]{2,1,0:T(8,128)(2,1)} reshape(bf16[320,2048]{1,0:T(8,128)(2,1)} %convolution_convert_fusion.1) | data formatting | bytes 2621440 | tf_op jit(solution)/shard_map/reshape | solution.py:26
  16.3 7.7 %all-to-all-start = ((bf16[32,10,2048]{2,1,0:T(8,128)(2,1)}), bf16[32,10,2048]{2,1,0:T(8,128)(2,1)}, u32[]{:S(2)}, u32[]{:S(2)}) async-start(bf16[32,10,2048]{2,1,0:T(8,128)(2,1)} %reshape.59), calls=%async_computation | async-start | bytes 4194304 | tf_op jit(solution)/shard_map/all_to_all | solution.py:29
  24.0 2.7 convolution_convert_fusion
  26.7 3.3 %reshape.61 = bf16[32,10,2048]{2,1,0:T(8,128)(2,1)} reshape(bf16[320,2048]{1,0:T(8,128)(2,1)} %convolution_convert_fusion) | data formatting | bytes 2621440 | tf_op jit(solution)/shard_map/reshape | solution.py:28
  30.0 22.0 %all-to-all-done = bf16[32,10,2048]{2,1,0:T(8,128)(2,1)} async-done(((bf16[32,10,2048]{2,1,0:T(8,128)(2,1)}), bf16[32,10,2048]{2,1,0:T(8,128)(2,1)}, u32[]{:S(2)}, u32[]{:S(2)}) %all-to-all-start) | async-done | bytes 1310752 | tf_op jit(solution)/shard_map/all_to_all | solution.py:29
  51.9 6.7 %all-to-all-start.2 = ((bf16[32,10,2048]{2,1,0:T(8,128)(2,1)}), bf16[32,10,2048]{2,1,0:T(8,128)(2,1)}, u32[]{:S(2)}, u32[]{:S(2)}) async-start(bf16[32,10,2048]{2,1,0:T(8,128)(2,1)} %reshape.61), calls=%async_computation.2 | async-start | bytes 4194304 | tf_op jit(solution)/shard_map/all_to_all | solution.py:43
  58.6 0.0 reduce-scatter.5.cloned.1.call-start
  58.7 0.0 copy-start.8
  58.7 4.5 %fusion.8 = f32[32,10,768]{2,0,1:T(8,128)S(1)} fusion(bf16[1,2048,768]{2,1,0:T(8,128)(2,1)} %param.8, bf16[32,10,2048]{2,1,0:T(8,128)(2,1)} %all-to-all-done), kind=kOutput, calls=%fused_computation.9 | convolution fusion | flops 1006632960 | bytes 5439488 | tf_op jit(solution)/shard_map/pcd,df->pcf/dot_general | solution.py:30
  63.2 0.0 copy-start.4
  63.2 0.9 copy-done.4
  64.2 0.0 copy-done.8
  64.2 4.6 %multiply_convert_fusion.2 = (bf16[32,10,768]{2,0,1:T(8,128)(2,1)}, f32[32,10,768]{2,0,1:T(8,128)}) fusion(f32[32,10,768]{2,0,1:T(8,128)S(1)} %fusion.8, bf16[1,2048,768]{2,1,0:T(8,128)(2,1)S(1)} %copy-done.8, bf16[32,10,2048]{2,1,0:T(8,128)(2,1)} %all-to-all-done), kind=kOutput, calls=%fused_computation.28 | convolution fusion | flops 1008107520 | bytes 6914048 | tf_op jit(solution)/shard_map/pcd,df->pcf/dot_general | solution.py:31
  68.8 17.9 %all-to-all-done.2 = bf16[32,10,2048]{2,1,0:T(8,128)(2,1)} async-done(((bf16[32,10,2048]{2,1,0:T(8,128)(2,1)}), bf16[32,10,2048]{2,1,0:T(8,128)(2,1)}, u32[]{:S(2)}, u32[]{:S(2)}) %all-to-all-start.2) | async-done | bytes 1310752 | tf_op jit(solution)/shard_map/all_to_all | solution.py:43
  86.7 6.4 %convolution_bitcast_fusion = f32[768,2048]{1,0:T(8,128)} fusion(bf16[32,10,768]{2,0,1:T(8,128)(2,1)} %get-tuple-element.9, bf16[32,10,2048]{2,1,0:T(8,128)(2,1)} %all-to-all-done.2), kind=kOutput, calls=%fused_computation | convolution fusion | flops 1006632960 | bytes 8093696 | tf_op jit(solution)/shard_map/sr,sd->rd/dot_general | solution.py:73
  93.0 0.0 reduce-scatter.5.cloned.1.call-update
  93.0 0.2 reduce-scatter.3.cloned.1.call-start
  93.3 0.0 copy-start.3
  93.3 3.1 copy.28
  96.3 0.0 copy-done.3
  96.3 1.8 copy.27
  98.1 2.5 reshape.63
  100.6 2.4 reshape.64
  103.0 3.6 %reshape.62 = bf16[320,2048]{1,0:T(8,128)(2,1)} reshape(bf16[32,10,2048]{2,1,0:T(8,128)(2,1)} %all-to-all-done.2) | data formatting | bytes 2621440 | tf_op jit(solution)/shard_map/reshape | solution.py:44
  106.7 3.6 %reshape.67 = bf16[320,2048]{1,0:T(8,128)(2,1)} reshape(bf16[32,10,2048]{2,1,0:T(8,128)(2,1)} %all-to-all-done) | data formatting | bytes 2621440 | tf_op jit(solution)/shard_map/reshape | solution.py:38
  110.2 0.0 copy-done
  110.2 0.0 copy-start.1
  110.2 3.5 %multiply_convert_fusion.1 = (bf16[320,768]{1,0:T(8,128)(2,1)S(1)}, bf16[320,768]{1,0:T(8,128)(2,1)S(1)}) fusion(f32[320,768]{1,0:T(8,128)} %reshape.64, f32[320,768]{1,0:T(8,128)} %reshape.63, bf16[320,2048]{1,0:T(8,128)(2,1)} %reshape.62, bf16[1,768,2048]{2,1,0:T(8,128)(2,1)S(1)} %copy-done), kind=kOutput, calls=%fused_computation.26 | convolution fusion | flops 1009827840 | bytes 7405568 | tf_op jit(solution)/shard_map/sd,fd->sf/dot_general | solution.py:45
  113.7 0.0 copy-start.5
  113.7 0.0 copy-start.7
  113.7 0.8 copy-done.5
  114.5 0.2 copy-done.7
  114.6 0.0 copy-done.1
  114.6 6.6 %fusion.22 = f32[2048,1536]{1,0:T(8,128)} fusion(bf16[320,2048]{1,0:T(8,128)(2,1)S(1)} %copy-done.1, bf16[320,768]{1,0:T(8,128)(2,1)S(1)} %get-tuple-element.6, bf16[320,768]{1,0:T(8,128)(2,1)S(1)} %get-tuple-element.5), kind=kOutput, calls=%fused_computation.21 | convolution fusion | flops 2015232000 | bytes 14876672 | tf_op jit(solution)/shard_map/sr,sf->rf/dot_general | solution.py:66
  121.3 0.0 reduce-scatter.3.cloned.1.call-update
  121.3 2.2 fusion.18
  123.5 2.1 copy.26
  125.6 6.7 %all-to-all-start.1 = ((bf16[32,10,2048]{2,1,0:T(8,128)(2,1)}), bf16[32,10,2048]{2,1,0:T(8,128)(2,1)}, u32[]{:S(2)}, u32[]{:S(2)}) async-start(bf16[32,10,2048]{2,1,0:T(8,128)(2,1)} %copy.26), calls=%async_computation.1 | async-start | bytes 4194304 | tf_op jit(solution)/shard_map/all_to_all | solution.py:36
  132.3 0.0 copy-start.6
  132.4 0.0 copy-start.9
  132.4 3.4 %fusion.6 = f32[320,2048]{1,0:T(8,128)S(1)} fusion(bf16[320,768]{1,0:T(8,128)(2,1)} %copy-done.7, bf16[1,2048,768]{2,1,0:T(8,128)(2,1)} %param.9), kind=kOutput, calls=%fused_computation.7 | convolution fusion | flops 1006632960 | bytes 6258688 | tf_op jit(solution)/shard_map/sf,df->sd/dot_general | solution.py:51
  135.8 0.0 copy-done.6
  135.8 0.0 copy-done.9
  135.8 2.3 fusion.15
  138.1 3.4 %reshape.65 = bf16[32,10,2048]{2,1,0:T(8,128)(2,1)} reshape(bf16[320,2048]{1,0:T(8,128)(2,1)} %fusion.15) | data formatting | bytes 2621440 | tf_op jit(solution)/shard_map/reshape | solution.py:54
  141.5 18.9 %all-to-all-done.1 = bf16[32,10,2048]{2,1,0:T(8,128)(2,1)} async-done(((bf16[32,10,2048]{2,1,0:T(8,128)(2,1)}), bf16[32,10,2048]{2,1,0:T(8,128)(2,1)}, u32[]{:S(2)}, u32[]{:S(2)}) %all-to-all-start.1) | async-done | bytes 1310752 | tf_op jit(solution)/shard_map/all_to_all | solution.py:36
  160.4 6.7 %all-to-all-start.3 = ((bf16[32,10,2048]{2,1,0:T(8,128)(2,1)}), bf16[32,10,2048]{2,1,0:T(8,128)(2,1)}, u32[]{:S(2)}, u32[]{:S(2)}) async-start(bf16[32,10,2048]{2,1,0:T(8,128)(2,1)} %reshape.65), calls=%async_computation.3 | async-start | bytes 4194304 | tf_op jit(solution)/shard_map/all_to_all | solution.py:53
  167.1 3.6 %reshape.60 = bf16[320,2048]{1,0:T(8,128)(2,1)} reshape(bf16[32,10,2048]{2,1,0:T(8,128)(2,1)} %all-to-all-done.1) | data formatting | bytes 2621440 | tf_op jit(solution)/shard_map/reshape | solution.py:37
  170.7 24.4 %all-to-all-done.3 = bf16[32,10,2048]{2,1,0:T(8,128)(2,1)} async-done(((bf16[32,10,2048]{2,1,0:T(8,128)(2,1)}), bf16[32,10,2048]{2,1,0:T(8,128)(2,1)}, u32[]{:S(2)}, u32[]{:S(2)}) %all-to-all-start.3) | async-done | bytes 1310752 | tf_op jit(solution)/shard_map/all_to_all | solution.py:53
  195.1 3.6 %reshape.66 = bf16[320,2048]{1,0:T(8,128)(2,1)} reshape(bf16[32,10,2048]{2,1,0:T(8,128)(2,1)} %all-to-all-done.3) | data formatting | bytes 2621440 | tf_op jit(solution)/shard_map/reshape | solution.py:56
  198.7 2.9 convolution_convert_fusion.3
  201.5 0.0 copy-done.2
  201.5 1.4 convolution_convert_fusion.2
  202.9 2.0 fusion.30
  204.9 99.5 %reduce-scatter.3.cloned.1.call-done = f32[256,1536]{1,0:T(8,128)} async-done(((f32[2048,1536]{1,0:T(8,128)}), f32[256,1536]{1,0:T(8,128)}) %reduce-scatter.3.cloned.1.call-update) | async-done | bytes 1572880 | tf_op jit(solution)/shard_map/reduce_scatter | solution.py:65
  304.4 2.4 fusion.32
  (5 shorter events, 0.1 us)
Async XLA Ops:
  7.2 103.1 %copy-start = (bf16[1,768,2048]{2,1,0:T(8,128)(2,1)S(1)}, bf16[1,768,2048]{2,1,0:T(8,128)(2,1)}, u32[]{:S(2)}) copy-start(bf16[1,768,2048]{2,1,0:T(8,128)(2,1)} %param.10) | copy-start | bytes 9437188
  16.3 35.6 %all-to-all-start = ((bf16[32,10,2048]{2,1,0:T(8,128)(2,1)}), bf16[32,10,2048]{2,1,0:T(8,128)(2,1)}, u32[]{:S(2)}, u32[]{:S(2)}) async-start(bf16[32,10,2048]{2,1,0:T(8,128)(2,1)} %reshape.59), calls=%async_computation | async-start | bytes 4194304 | tf_op jit(solution)/shard_map/all_to_all | solution.py:29
  51.9 34.7 %all-to-all-start.2 = ((bf16[32,10,2048]{2,1,0:T(8,128)(2,1)}), bf16[32,10,2048]{2,1,0:T(8,128)(2,1)}, u32[]{:S(2)}, u32[]{:S(2)}) async-start(bf16[32,10,2048]{2,1,0:T(8,128)(2,1)} %reshape.61), calls=%async_computation.2 | async-start | bytes 4194304 | tf_op jit(solution)/shard_map/all_to_all | solution.py:43
  58.6 144.3 %reduce-scatter.5.cloned.1.call-start = ((), (), s32[]{:S(2)}) async-start(), calls=%async_computation.7 | async-start | bytes 7077888 | tf_op jit(solution)/shard_map/reduce_scatter | solution.py:72
  58.7 5.5 %copy-start.8 = (bf16[1,2048,768]{2,1,0:T(8,128)(2,1)S(1)}, bf16[1,2048,768]{2,1,0:T(8,128)(2,1)}, u32[]{:S(2)}) copy-start(bf16[1,2048,768]{2,1,0:T(8,128)(2,1)} %param.9) | copy-start | bytes 9437188
  63.2 1.0 copy-start.4
  93.0 211.4 %reduce-scatter.3.cloned.1.call-start = ((), (), s32[]{:S(2)}) async-start(), calls=%async_computation.6 | async-start | bytes 14155776 | tf_op jit(solution)/shard_map/reduce_scatter | solution.py:65
  93.3 3.1 copy-start.3
  110.2 4.4 %copy-start.1 = (bf16[320,2048]{1,0:T(8,128)(2,1)S(1)}, bf16[320,2048]{1,0:T(8,128)(2,1)}, u32[]{:S(2)}) copy-start(bf16[320,2048]{1,0:T(8,128)(2,1)} %reshape.67) | copy-start | bytes 3932164
  113.7 0.8 copy-start.5
  113.7 0.9 copy-start.7
  125.6 34.7 %all-to-all-start.1 = ((bf16[32,10,2048]{2,1,0:T(8,128)(2,1)}), bf16[32,10,2048]{2,1,0:T(8,128)(2,1)}, u32[]{:S(2)}, u32[]{:S(2)}) async-start(bf16[32,10,2048]{2,1,0:T(8,128)(2,1)} %copy.26), calls=%async_computation.1 | async-start | bytes 4194304 | tf_op jit(solution)/shard_map/all_to_all | solution.py:36
  132.3 3.5 %copy-start.6 = (bf16[320,768]{1,0:T(8,128)(2,1)S(1)}, bf16[320,768]{1,0:T(8,128)(2,1)}, u32[]{:S(2)}) copy-start(bf16[320,768]{1,0:T(8,128)(2,1)} %copy-done.5) | copy-start | bytes 1474564
  132.4 3.5 %copy-start.9 = (bf16[1,2048,768]{2,1,0:T(8,128)(2,1)S(1)}, bf16[1,2048,768]{2,1,0:T(8,128)(2,1)}, u32[]{:S(2)}) copy-start(bf16[1,2048,768]{2,1,0:T(8,128)(2,1)} %param.8) | copy-start | bytes 9437188
  160.4 34.7 %all-to-all-start.3 = ((bf16[32,10,2048]{2,1,0:T(8,128)(2,1)}), bf16[32,10,2048]{2,1,0:T(8,128)(2,1)}, u32[]{:S(2)}, u32[]{:S(2)}) async-start(bf16[32,10,2048]{2,1,0:T(8,128)(2,1)} %reshape.65), calls=%async_computation.3 | async-start | bytes 4194304 | tf_op jit(solution)/shard_map/all_to_all | solution.py:53
  198.7 2.9 copy-start.2
Sparse Core Ops, SparseCore 0:
  93.2 75.4 reduce-scatter.4
  171.2 133.1 reduce-scatter.2
where the time goes:
time: 316 us; the launch traced here: 314 us
  waiting for transfers between devices  183 us (58%)
  matrix products  43.1 us (14%)
  local copies, waits for them, and re-layouts  38.4 us (12%)
  starting transfers between devices  28 us (9%)
  between operations  14.2 us (4%)
  other arithmetic  7.3 us (2%)
    reduce_scatter x1, waiting for transfers between devices, shards(): lax.psum_scatter(jnp.einsum('sr,sf->rf', columns, both_grads, preferred_e...  99.5 us
    all_to_all x1, waiting for transfers between devices, shards(): lax.all_to_all(input_grad.reshape(peers, slots, width), 'expert', split_a...  24.4 us
    all_to_all x1, waiting for transfers between devices, shards(): lax.all_to_all(outgoing, 'expert', split_axis=0, concat_axis=0, tiled=True)  22 us
    all_to_all x1, waiting for transfers between devices, shards(): lax.all_to_all(result, 'expert', split_axis=0, concat_axis=0, tiled=True)  18.9 us
    all_to_all x1, waiting for transfers between devices, shards(): lax.all_to_all(send_grad, 'expert', split_axis=0, concat_axis=0, tiled=True)  17.9 us
    all_to_all x1, starting transfers between devices, shards(): lax.all_to_all(outgoing, 'expert', split_axis=0, concat_axis=0, tiled=True)  7.67 us
    all_to_all x1, starting transfers between devices, shards(): lax.all_to_all(send_grad, 'expert', split_axis=0, concat_axis=0, tiled=True)  6.7 us
    all_to_all x1, starting transfers between devices, shards(): lax.all_to_all(result, 'expert', split_axis=0, concat_axis=0, tiled=True)  6.7 us
  transfers between devices with their start and end apart: 6, of which 5 were waited for; matrix products, arithmetic and copies ran while one was open for 22% of the time, Pallas kernels for 0%

commit v1 on v0

v1 whole, which is shorter than its diff:
```python
import functools

import jax
import jax.numpy as jnp
from jax import lax
from jax.experimental import pallas as pl
from jax.experimental.pallas import tpu as pltpu
from jax.sharding import PartitionSpec as P

F32 = jnp.float32
BF16 = jnp.bfloat16
MAIN = 8
QUARTERS = 4
VMEM_LIMIT = 56 * 1024 * 1024


def mm(a, b, dims):
    return lax.dot_general(a, b, (dims, ((), ())), preferred_element_type=F32)


NN = ((1,), (0,))
NT = ((1,), (1,))
TN = ((0,), (0,))


def params():
    return pltpu.CompilerParams(vmem_limit_bytes=VMEM_LIMIT)


def iota(shape, dim):
    return lax.broadcasted_iota(jnp.int32, shape, dim)


def as_row(col):
    wide = jnp.broadcast_to(col.astype(F32), (col.shape[0], 128))
    return jnp.transpose(wide)[0:1, :].astype(jnp.int32)


def mask(cond):
    return jnp.where(cond, 1.0, 0.0).astype(BF16)


def pack_kernel(rows, width, peers, exp_ref, tok_ref, gout_ref, out_ref):
    col = exp_ref[...]
    row = as_row(col)
    earlier = (col == row) & (iota((rows, rows), 0) < iota((rows, rows), 1))
    rank = jnp.sum(jnp.where(earlier, 1.0, 0.0), axis=0, keepdims=True).astype(jnp.int32)
    slots = peers * MAIN
    r = iota((slots, rows), 0)
    here = (r >> 3) == row
    whole = mask(here & ((r & 7) == rank))
    late = here & (((r >> 2) & 1) + MAIN == rank)
    part = width // QUARTERS
    both = width + part
    for k, src in enumerate((tok_ref, gout_ref)):
        at = k * both
        out_ref[:, at : at + width] = mm(whole, src[...], NN).astype(BF16)
        tail = jnp.zeros((slots, part), F32)
        for q in range(QUARTERS):
            tail += mm(mask(late & ((r & 3) == q)), src[:, q * part : (q + 1) * part], NN)
        out_ref[:, at + width : at + both] = tail.astype(BF16)


def pack(expert_of, tokens, grad_out, peers):
    rows, width = tokens.shape
    return pl.pallas_call(
        functools.partial(pack_kernel, rows, width, peers),
        out_shape=jax.ShapeDtypeStruct((peers * MAIN, 2 * (width + width // QUARTERS)), BF16),
        compiler_params=params(),
        name="pack",
    )(expert_of, tokens, grad_out)


def unpack_kernel(rows, width, peers, exp_ref, back_ref, mixed_ref, gtok_ref):
    col = exp_ref[...]
    row = as_row(col)
    earlier = (col == row) & (iota((rows, rows), 1) < iota((rows, rows), 0))
    rank = jnp.sum(jnp.where(earlier, 1.0, 0.0), axis=1, keepdims=True).astype(jnp.int32)
    slots = peers * MAIN
    r = iota((rows, slots), 1)
    here = (r >> 3) == col
    whole = mask(here & ((r & 7) == rank))
    late = here & (((r >> 2) & 1) + MAIN == rank)
    part = width // QUARTERS
    both = width + part
    for k, dst in enumerate((mixed_ref, gtok_ref)):
        at = k * both
        tail = back_ref[:, at + width : at + both]
        for q in range(QUARTERS):
            got = mm(whole, back_ref[:, at + q * part : at + (q + 1) * part], NN)
            got += mm(mask(late & ((r & 3) == q)), tail, NN)
            dst[:, q * part : (q + 1) * part] = got.astype(BF16)


def unpack(expert_of, back, rows, width, peers):
    out = jax.ShapeDtypeStruct((rows, width), BF16)
    return pl.pallas_call(
        functools.partial(unpack_kernel, rows, width, peers),
        out_shape=(out, out),
        compiler_params=params(),
        name="unpack",
    )(expert_of, back)


def picks(slots, tails, q):
    return mask(iota((tails, slots), 1) == iota((tails, slots), 0) * QUARTERS + q)


def hidden_kernel(scale, recv_ref, wg_ref, wu_ref, wd_ref, x_ref, act_ref, gg_ref, gu_ref, down_ref, dy_ref):
    slots = recv_ref.shape[0]
    width = x_ref.shape[1]
    part = width // QUARTERS
    tails = slots // QUARTERS

    @pl.when(pl.program_id(0) == 0)
    def _():
        for k, dst in enumerate((x_ref, dy_ref)):
            at = k * (width + part)
            dst[0:slots, :] = recv_ref[:, at : at + width]
            tail = recv_ref[:, at + width : at + width + part]
            for q in range(QUARTERS):
                dst[slots : slots + tails, q * part : (q + 1) * part] = mm(
                    picks(slots, tails, q), tail, NN
                ).astype(BF16)

    x = x_ref[...]
    dy = dy_ref[...]
    gate = mm(x, wg_ref[...], NN)
    up = mm(x, wu_ref[...], NN)
    sig = jax.nn.sigmoid(gate)
    swish = gate * sig
    act = (swish * up).astype(BF16)
    act_ref[...] = act
    down_ref[...] = (mm(act, dy, TN) * scale).astype(BF16)
    grad_act = mm(dy, wd_ref[...], NT)
    gg_ref[...] = (grad_act * up * sig * (1.0 + gate * (1.0 - sig))).astype(BF16)
    gu_ref[...] = (grad_act * swish).astype(BF16)


def hidden(recv, wg, wu, wd, scale, tile=256):
    slots = recv.shape[0]
    width, inner = wg.shape
    total = slots + slots // QUARTERS
    cols = pl.BlockSpec((width, tile), lambda i: (0, i))
    rows = pl.BlockSpec((tile, width), lambda i: (i, 0))
    slab = pl.BlockSpec((total, tile), lambda i: (0, i))
    mid = jax.ShapeDtypeStruct((total, inner), BF16)
    return pl.pallas_call(
        functools.partial(hidden_kernel, scale),
        grid=(inner // tile,),
        in_specs=[pl.BlockSpec(recv.shape, lambda i: (0, 0)), cols, cols, rows],
        out_specs=[pl.BlockSpec((total, width), lambda i: (0, 0)), slab, slab, slab, rows],
        out_shape=[
            jax.ShapeDtypeStruct((total, width), BF16),
            mid,
            mid,
            mid,
            jax.ShapeDtypeStruct((inner, width), BF16),
        ],
        scratch_shapes=[pltpu.VMEM((total, width), BF16)],
        compiler_params=params(),
        cost_estimate=pl.CostEstimate(
            flops=8 * total * width * inner, bytes_accessed=8 * width * inner, transcendentals=total * inner
        ),
        name="hidden",
    )(recv, wg, wu, wd)


def outer_kernel(scale, x_ref, gg_ref, gu_ref, gate_ref, up_ref):
    x = x_ref[...]
    gate_ref[0] = (mm(x, gg_ref[...], TN) * scale).astype(BF16)
    up_ref[0] = (mm(x, gu_ref[...], TN) * scale).astype(BF16)


def outer(x, gg, gu, scale, groups):
    total, width = x.shape
    inner = gg.shape[1]
    rows = width // groups
    whole = pl.BlockSpec((total, inner), lambda i: (0, 0))
    piece = pl.BlockSpec((1, rows, inner), lambda i: (i, 0, 0))
    out = jax.ShapeDtypeStruct((groups, rows, inner), BF16)
    return pl.pallas_call(
        functools.partial(outer_kernel, scale),
        grid=(groups,),
        in_specs=[pl.BlockSpec((total, rows), lambda i: (0, i)), whole, whole],
        out_specs=[piece, piece],
        out_shape=[out, out],
        compiler_params=params(),
        cost_estimate=pl.CostEstimate(
            flops=4 * total * width * inner, bytes_accessed=4 * width * inner, transcendentals=0
        ),
        name="outer",
    )(x, gg, gu)


def rows_kernel(act_ref, gg_ref, gu_ref, wg_ref, wu_ref, wd_ref, out_ref):
    step = pl.program_id(0)
    slots = out_ref.shape[0]
    part = wd_ref.shape[1]
    width = part * QUARTERS
    both = width + part
    tails = slots // QUARTERS
    mixed = mm(act_ref[...], wd_ref[...], NN).astype(BF16)
    gtok = (mm(gg_ref[...], wg_ref[...], NT) + mm(gu_ref[...], wu_ref[...], NT)).astype(BF16)
    pick = mask(iota((slots, tails), 0) == iota((slots, tails), 1) * QUARTERS + step)
    mine = (iota((slots, part), 0) & (QUARTERS - 1)) == step
    for k, val in enumerate((mixed, gtok)):
        at = pl.multiple_of(k * both + step * part, 128)
        out_ref[:, pl.ds(at, part)] = val[0:slots, :]
        tail = mm(pick, val[slots : slots + tails, :], NN).astype(BF16)
        lo = k * both + width
        out_ref[:, lo : lo + part] = jnp.where(mine, tail, out_ref[:, lo : lo + part])


def rows_back(act, gg, gu, wg, wu, wd):
    total, inner = act.shape
    width = wg.shape[0]
    slots = total * QUARTERS // (QUARTERS + 1)
    part = width // QUARTERS
    whole = pl.BlockSpec((total, inner), lambda i: (0, 0))
    wrow = pl.BlockSpec((part, inner), lambda i: (i, 0))
    out = (slots, 2 * (width + part))
    return pl.pallas_call(
        rows_kernel,
        grid=(QUARTERS,),
        in_specs=[whole, whole, whole, wrow, wrow, pl.BlockSpec((inner, part), lambda i: (0, i))],
        out_specs=pl.BlockSpec(out, lambda i: (0, 0)),
        out_shape=jax.ShapeDtypeStruct(out, BF16),
        compiler_params=params(),
        cost_estimate=pl.CostEstimate(
            flops=6 * total * width * inner, bytes_accessed=6 * width * inner, transcendentals=0
        ),
        name="rows_back",
    )(act, gg, gu, wg, wu, wd)


def ring_sums(tensors):
    groups = tensors[0].shape[0]
    z = lax.axis_index("dp")
    right = [(i, (i + 1) % groups) for i in range(groups)]
    left = [(i, (i - 1) % groups) for i in range(groups)]

    def own(parts, d):
        return lax.dynamic_index_in_dim(parts, (z + d) % groups, 0, keepdims=False)

    def add(a, b):
        return (a.astype(F32) + b.astype(F32)).astype(BF16)

    def send(r, l):
        return lax.ppermute(r, "dp", right), lax.ppermute(l, "dp", left)

    far = groups // 2
    halves = [parts.shape[1] // 2 for parts in tensors]
    moving = [send(own(p, far)[:h], own(p, far)[h:]) for p, h in zip(tensors, halves)]
    for d in range(far - 1, 0, -1):
        for k, (p, h) in enumerate(zip(tensors, halves)):
            r, l = moving[k]
            a, b = own(p, d), own(p, -d)
            if d == far - 1:
                r = jnp.concatenate([add(a[:h], r), a[h:]], 0)
                l = jnp.concatenate([b[:h], add(b[h:], l)], 0)
            else:
                r, l = add(a, r), add(b, l)
            moving[k] = send(r, l)
    return [
        (own(p, 0).astype(F32) + r.astype(F32) + l.astype(F32)).astype(BF16)
        for p, (r, l) in zip(tensors, moving)
    ]


def shards(tokens, expert_of, w_gate, w_up, w_down, grad_out):
    rows, width = tokens.shape
    peers = lax.axis_size("expert")
    groups = lax.axis_size("dp")
    wg, wu, wd = w_gate[0], w_up[0], w_down[0]
    inner = wg.shape[1]
    scale = float(rows * groups) ** (-0.5)

    def exchange(packed):
        swapped = lax.all_to_all(
            packed.reshape(peers, MAIN, -1), "expert", split_axis=0, concat_axis=0, tiled=True
        )
        return swapped.reshape(peers * MAIN, -1)

    recv = exchange(pack(expert_of, tokens, grad_out, peers))
    x, act, gg, gu, down = hidden(recv, wg, wu, wd, scale)
    gate, up = outer(x, gg, gu, scale, groups)
    grad_down, grad_gate, grad_up = ring_sums([down.reshape(groups, inner // groups, width), gate, up])
    back = exchange(rows_back(act, gg, gu, wg, wu, wd))
    mixed, grad_tokens = unpack(expert_of, back, rows, width, peers)
    return mixed, grad_tokens, grad_gate[None], grad_up[None], grad_down[None]


def solution(mesh):
    in_specs = (
        P(("dp", "expert"), None),
        P(("dp", "expert"), None),
        P("expert", None, None),
        P("expert", None, None),
        P("expert", None, None),
        P(("dp", "expert"), None),
    )
    out_specs = (
        P(("dp", "expert"), None),
        P(("dp", "expert"), None),
        P("expert", "dp", None),
        P("expert", "dp", None),
        P("expert", "dp", None),
    )
    return jax.shard_map(shards, mesh=mesh, in_specs=in_specs, out_specs=out_specs, check_vma=False)
```

time: 316 us -> 207 us (0.66)
  waiting for transfers between devices: 183 us -> 109 us
  matrix products: 43.1 us -> 0 us
  Pallas kernels: 0 us -> 37.6 us
  local copies, waits for them, and re-layouts: 38.4 us -> 10.6 us
  between operations: 14.2 us -> 1.01 us
  starting transfers between devices: 28 us -> 38.2 us
    reduce_scatter x2 -> x0, waiting for transfers between devices: 99.5 us -> none  [the longest x1 99.5 us: shards(): lax.psum_scatter(jnp.einsum('sr,sf->rf', columns, both_grads, preferred_e...]
    ppermute x0 -> x24, waiting for transfers between devices: none -> 75.4 us  [send(): return (lax.ppermute(r, 'dp', right), lax.ppermute(l, 'dp', left))]
    all_to_all x4 -> x2, waiting for transfers between devices: 83.1 us -> 33.7 us  [exchange(): lax.all_to_all(packed.reshape(peers, MAIN, -1), 'expert', split_axis=0, c...]
    dot_general x12 -> x0, matrix products: 43.1 us -> none  [the longest x1 6.63 us: shards(): jnp.einsum('sr,sf->rf', columns, both_grads, preferred_element_type=jnp.f...]
    pallas_call x0 -> x5, Pallas kernels: none -> 37.6 us  [the longest x1 12.3 us: hidden(): pl.pallas_call(functools.partial(hidden_kernel, scale), grid=(inner // ti...]
    reshape x9 -> x0, local copies, waits for them, and re-layouts: 29.3 us -> none  [the longest x1 3.64 us: shards(): arriving = arriving.reshape(peers * slots, width)]
    ppermute x0 -> x24, starting transfers between devices: none -> 24.4 us  [send(): return (lax.ppermute(r, 'dp', right), lax.ppermute(l, 'dp', left))]
    all_to_all x4 -> x2, starting transfers between devices: 27.8 us -> 13.8 us  [exchange(): lax.all_to_all(packed.reshape(peers, MAIN, -1), 'expert', split_axis=0, c...]
  transfers between devices with their start and end apart: 6 -> 26, of which waited for: 5 -> 12; matrix products, arithmetic and copies ran while one was open for 22% -> 7% of each run, Pallas kernels for 0% -> 8%
where the time goes in v1:
time: 207 us; the launch traced here: 206 us
  waiting for transfers between devices  109 us (53%)
  starting transfers between devices  38.2 us (18%)
  Pallas kernels  37.6 us (18%)
  local copies, waits for them, and re-layouts  10.6 us (5%)
  other arithmetic  9.91 us (5%)
    ppermute x24, waiting for transfers between devices, send(): return (lax.ppermute(r, 'dp', right), lax.ppermute(l, 'dp', left))  75.4 us
    all_to_all x2, waiting for transfers between devices, exchange(): lax.all_to_all(packed.reshape(peers, MAIN, -1), 'expert', split_axis=0, c...  33.7 us
    ppermute x24, starting transfers between devices, send(): return (lax.ppermute(r, 'dp', right), lax.ppermute(l, 'dp', left))  24.4 us
    all_to_all x2, starting transfers between devices, exchange(): lax.all_to_all(packed.reshape(peers, MAIN, -1), 'expert', split_axis=0, c...  13.8 us
    pallas_call x1, Pallas kernels, hidden(): pl.pallas_call(functools.partial(hidden_kernel, scale), grid=(inner // ti...  12.3 us
    pallas_call x1, Pallas kernels, rows_back(): pl.pallas_call(rows_kernel, grid=(QUARTERS,), in_specs=[whole, whole, who...  8.95 us
    pallas_call x1, Pallas kernels, outer(): pl.pallas_call(functools.partial(outer_kernel, scale), grid=(groups,), in...  8.34 us
    slice x3, local copies, waits for them, and re-layouts, ring_sums(): own(p, far)[:h]  6.16 us
  transfers between devices with their start and end apart: 26, of which 12 were waited for; matrix products, arithmetic and copies ran while one was open for 7% of the time, Pallas kernels for 8%

profile of v1, /device:TPU:2, one launch (start us, length us, event | category | flops | bytes accessed | tf_op | source)
XLA Modules:
  0.0 206.4 jit_solution(101444511412466703)
XLA Ops:
  0.6 1.4 copy.12.exp_ref
  2.1 4.2 %pack.1 = bf16[256,5120]{1,0:T(8,128)(2,1)} custom-call(s32[160,1]{1,0:T(8,128)} %copy.12.exp_ref, bf16[160,2048]{1,0:T(8,128)(2,1)} %tok_ref.1, bf16[160,2048]{1,0:T(8,128)(2,1)} %gout_ref.1), custom_call_target="tpu_custom_call" | custom-call | tf_op jit(solution)/shard_map/pack/pallas_call | solution.py:66
  6.3 7.6 %all-to-all-start = ((bf16[32,8,5120]{2,1,0:T(8,128)(2,1)}), bf16[32,8,5120]{2,1,0:T(8,128)(2,1)S(1)}, u32[]{:S(2)}, u32[]{:S(2)}) async-start(bf16[32,8,5120]{2,1,0:T(8,128)(2,1)} %bitcast.115), calls=%async_computation | async-start | bytes 5242880 | tf_op jit(solution)/shard_map/all_to_all | solution.py:280
  14.0 33.7 %all-to-all-done = bf16[32,8,5120]{2,1,0:T(8,128)(2,1)S(1)} async-done(((bf16[32,8,5120]{2,1,0:T(8,128)(2,1)}), bf16[32,8,5120]{2,1,0:T(8,128)(2,1)S(1)}, u32[]{:S(2)}, u32[]{:S(2)}) %all-to-all-start) | async-done | bytes 2621472 | tf_op jit(solution)/shard_map/all_to_all | solution.py:280
  47.7 1.5 copy-done.4
  49.2 12.3 %hidden.1 = (bf16[320,2048]{1,0:T(8,128)(2,1)}, bf16[320,768]{1,0:T(8,128)(2,1)}, bf16[320,768]{1,0:T(8,128)(2,1)}, bf16[320,768]{1,0:T(8,128)(2,1)}, bf16[768,2048]{1,0:T(8,128)(2,1)}) custom-call(bf16[256,5120]{1,0:T(8,128)(2,1)} %bitcast.128, bf16[2048,768]{1,0:T(8,128)(2,1)} %bitcast.122, bf16[2048,768]{1,0:T(8,128)(2,1)} %bitcast.124, ...), custom_call_target="tpu_custom_call" | custom-call | flops 4026531840 | bytes 12582912 | tf_op jit(solution)/shard_map/hidden/pallas_call | solution.py:148
  61.6 2.1 %dynamic-slice_bitcast_fusion.4 = (bf16[48,2048]{1,0:T(8,128)(2,1)}, bf16[48,2048]{1,0:T(8,128)(2,1)}, bf16[48,2048]{1,0:T(8,128)(2,1)}, bf16[48,2048]{1,0:T(8,128)(2,1)}) fusion(bf16[8,96,2048]{2,1,0:T(8,128)(2,1)} %bitcast.116, s32[]{:T(128)S(6)} %select_n.127, s32[]{:T(128)S(6)} %select_n.133, s32[]{:T(128)S(6)} %add.252, s32[]{:T(128)S(6)} %select_n.125), kind=kLoop, calls=%fused_computation.58 | loop fusion | bytes 1572880 | tf_op jit(solution)/shard_map/slice | solution.py:254
  63.7 1.9 collective-permute-start.16
  65.6 3.9 %collective-permute-start.20 = (bf16[48,2048]{1,0:T(8,128)(2,1)}, bf16[48,2048]{1,0:T(8,128)(2,1)}, u32[]{:S(2)}, u32[]{:S(2)}) collective-permute-start(bf16[48,2048]{1,0:T(8,128)(2,1)} %get-tuple-element.29), channel_id=1, source_target_pairs={{0,224},{32,0},{64,32},{96,64},{128,96},{160,128},{192,160},{224,1... | collective-permute-start | bytes 589832 | tf_op jit(solution)/shard_map/ppermute | solution.py:250
  69.6 8.3 %outer.1 = (bf16[8,256,768]{2,1,0:T(8,128)(2,1)}, bf16[8,256,768]{2,1,0:T(8,128)(2,1)}) custom-call(bf16[320,2048]{1,0:T(8,128)(2,1)} %get-tuple-element.19.x_ref, bf16[320,768]{1,0:T(8,128)(2,1)} %get-tuple-element.15.gg_ref, bf16[320,768]{1,0:T(8,128)(2,1)} %get-tuple-element.16.gu_ref), custom_call_target="tpu_custom_call" | custom-call | flops 2013265920 | bytes 6291456 | tf_op jit(solution)/shard_map/outer/pallas_call | solution.py:182
  77.9 2.0 dynamic-slice_bitcast_fusion.10
  79.9 2.0 collective-permute-start.12
  81.9 2.0 dynamic-slice_bitcast_fusion.16
  84.0 8.9 %rows_back.1 = bf16[256,5120]{1,0:T(8,128)(2,1)} custom-call(bf16[320,768]{1,0:T(8,128)(2,1)} %get-tuple-element.14.act_ref, bf16[320,768]{1,0:T(8,128)(2,1)} %get-tuple-element.15.gg_ref, bf16[320,768]{1,0:T(8,128)(2,1)} %get-tuple-element.16.gu_ref, bf16[2048,768]{1,0:T(8,128)(2,1)} %bitcast.123, bf16[2048,768]{1,0:T(8,128)(2,1)} %bitcast.125, ...), custom_call_target="tpu_custom_call" | custom-call | flops 3019898880 | bytes 9437184 | tf_op jit(solution)/shard_map/rows_back/pallas_call | solution.py:223
  92.9 6.2 %all-to-all-start.1 = ((bf16[32,8,5120]{2,1,0:T(8,128)(2,1)}), bf16[32,8,5120]{2,1,0:T(8,128)(2,1)S(1)}, u32[]{:S(2)}, u32[]{:S(2)}) async-start(bf16[32,8,5120]{2,1,0:T(8,128)(2,1)} %bitcast.113), calls=%async_computation.1 | async-start | bytes 5242880 | tf_op jit(solution)/shard_map/all_to_all | solution.py:280
  99.1 3.3 %collective-permute-start.4 = (bf16[128,768]{1,0:T(8,128)(2,1)}, bf16[128,768]{1,0:T(8,128)(2,1)S(1)}, u32[]{:S(2)}, u32[]{:S(2)}) collective-permute-start(bf16[128,768]{1,0:T(8,128)(2,1)} %get-tuple-element.45), channel_id=1, source_target_pairs={{0,224},{32,0},{64,32},{96,64},{128,96},{160,128},{192,160},{224,1... | collective-permute-start | bytes 589832 | tf_op jit(solution)/shard_map/ppermute | solution.py:250
  102.4 0.0 collective-permute-done.20
  102.4 1.3 fusion.22
  103.7 1.0 pad_maximum_fusion.5
  104.7 2.1 %collective-permute-start.21 = (bf16[96,2048]{1,0:T(8,128)(2,1)S(1)}, bf16[96,2048]{1,0:T(8,128)(2,1)S(1)}, u32[]{:S(2)}, u32[]{:S(2)}) collective-permute-start(bf16[96,2048]{1,0:T(8,128)(2,1)S(1)} %pad_maximum_fusion.5), channel_id=1, source_target_pairs={{0,224},{32,0},{64,32},{96,64},{128,96},{160,128},{192,160},{224,1... | collective-permute-start | bytes 1179656 | tf_op jit(solution)/shard_map/ppermute | solution.py:250
  106.8 1.1 pad_maximum_fusion.4
  107.9 0.0 collective-permute-done.12
  107.9 0.3 collective-permute-start.17
  108.2 0.0 collective-permute-done.8
  108.2 1.3 fusion.24
  109.5 0.1 collective-permute-start.9
  109.7 1.2 fusion.26
  110.9 1.0 collective-permute-start.1
  112.0 2.3 %collective-permute-start.13 = (bf16[256,768]{1,0:T(8,128)(2,1)S(1)}, bf16[256,768]{1,0:T(8,128)(2,1)S(1)}, u32[]{:S(2)}, u32[]{:S(2)}) collective-permute-start(bf16[256,768]{1,0:T(8,128)(2,1)S(1)} %pad_maximum_fusion.3), channel_id=1, source_target_pairs={{0,224},{32,0},{64,32},{96,64},{128,96},{160,128},{192,160},{224,1... | collective-permute-start | bytes 1179656 | tf_op jit(solution)/shard_map/ppermute | solution.py:250
  114.3 15.5 %collective-permute-done.9 = bf16[256,768]{1,0:T(8,128)(2,1)S(1)} collective-permute-done((bf16[256,768]{1,0:T(8,128)(2,1)S(1)}, bf16[256,768]{1,0:T(8,128)(2,1)S(1)}, u32[]{:S(2)}, u32[]{:S(2)}) %collective-permute-start.9) | collective-permute-done | bytes 393248 | tf_op jit(solution)/shard_map/ppermute | solution.py:250
  129.8 0.1 fusion.8
  129.9 6.9 %collective-permute-done.1 = bf16[256,768]{1,0:T(8,128)(2,1)S(1)} collective-permute-done((bf16[256,768]{1,0:T(8,128)(2,1)S(1)}, bf16[256,768]{1,0:T(8,128)(2,1)S(1)}, u32[]{:S(2)}, u32[]{:S(2)}) %collective-permute-start.1) | collective-permute-done | bytes 393248 | tf_op jit(solution)/shard_map/ppermute | solution.py:250
  136.8 0.1 fusion.14
  136.9 0.1 collective-permute-start.2
  137.0 0.1 fusion.2
  137.2 1.0 collective-permute-start.18
  138.2 11.9 %collective-permute-done.10 = bf16[256,768]{1,0:T(8,128)(2,1)S(1)} collective-permute-done((bf16[256,768]{1,0:T(8,128)(2,1)S(1)}, bf16[256,768]{1,0:T(8,128)(2,1)S(1)}, u32[]{:S(2)}, u32[]{:S(2)}) %collective-permute-start.10) | collective-permute-done | bytes 393248 | tf_op jit(solution)/shard_map/ppermute | solution.py:250
  150.1 0.2 fusion.9
  150.3 0.1 collective-permute-start.14
  150.4 8.1 %collective-permute-done.2 = bf16[256,768]{1,0:T(8,128)(2,1)S(1)} collective-permute-done((bf16[256,768]{1,0:T(8,128)(2,1)S(1)}, bf16[256,768]{1,0:T(8,128)(2,1)S(1)}, u32[]{:S(2)}, u32[]{:S(2)}) %collective-permute-start.2) | collective-permute-done | bytes 393248 | tf_op jit(solution)/shard_map/ppermute | solution.py:250
  158.5 0.2 fusion.15
  158.7 0.1 collective-permute-start.6
  158.8 5.8 %collective-permute-done.18 = bf16[96,2048]{1,0:T(8,128)(2,1)S(1)} collective-permute-done((bf16[96,2048]{1,0:T(8,128)(2,1)S(1)}, bf16[96,2048]{1,0:T(8,128)(2,1)S(1)}, u32[]{:S(2)}, u32[]{:S(2)}) %collective-permute-start.18) | collective-permute-done | bytes 393248 | tf_op jit(solution)/shard_map/ppermute | solution.py:250
  164.6 0.3 fusion.3
  164.9 0.1 collective-permute-start.22
  165.0 2.0 collective-permute-start.19
  167.0 0.0 collective-permute-start.11
  167.0 0.1 collective-permute-start.3
  167.1 0.1 fusion.7
  167.2 0.6 collective-permute-done.6
  167.7 2.7 %collective-permute-start.15 = (bf16[256,768]{1,0:T(8,128)(2,1)S(1)}, bf16[256,768]{1,0:T(8,128)(2,1)S(1)}, u32[]{:S(2)}, u32[]{:S(2)}) collective-permute-start(bf16[256,768]{1,0:T(8,128)(2,1)S(1)} %fusion.7), channel_id=1, source_target_pairs={{0,224},{32,0},{64,32},{96,64},{128,96},{160,128},{192,160},{224,1... | collective-permute-start | bytes 1179656 | tf_op jit(solution)/shard_map/ppermute | solution.py:250
  170.4 0.1 fusion.13
  170.5 6.4 %collective-permute-done.22 = bf16[96,2048]{1,0:T(8,128)(2,1)S(1)} collective-permute-done((bf16[96,2048]{1,0:T(8,128)(2,1)S(1)}, bf16[96,2048]{1,0:T(8,128)(2,1)S(1)}, u32[]{:S(2)}, u32[]{:S(2)}) %collective-permute-start.22) | collective-permute-done | bytes 393248 | tf_op jit(solution)/shard_map/ppermute | solution.py:250
  177.0 1.2 collective-permute-start.7
  178.2 0.1 fusion.1
  178.3 8.4 %collective-permute-done.11 = bf16[256,768]{1,0:T(8,128)(2,1)S(1)} collective-permute-done((bf16[256,768]{1,0:T(8,128)(2,1)S(1)}, bf16[256,768]{1,0:T(8,128)(2,1)S(1)}, u32[]{:S(2)}, u32[]{:S(2)}) %collective-permute-start.11) | collective-permute-done | bytes 393248 | tf_op jit(solution)/shard_map/ppermute | solution.py:250
  186.7 0.9 fusion.19
  187.6 4.3 %collective-permute-done.3 = bf16[256,768]{1,0:T(8,128)(2,1)S(1)} collective-permute-done((bf16[256,768]{1,0:T(8,128)(2,1)S(1)}, bf16[256,768]{1,0:T(8,128)(2,1)S(1)}, u32[]{:S(2)}, u32[]{:S(2)}) %collective-permute-start.3) | collective-permute-done | bytes 393248 | tf_op jit(solution)/shard_map/ppermute | solution.py:250
  191.9 2.0 collective-permute-done.7
  193.8 0.9 fusion.18
  194.7 5.5 %collective-permute-done.23 = bf16[96,2048]{1,0:T(8,128)(2,1)S(1)} collective-permute-done((bf16[96,2048]{1,0:T(8,128)(2,1)S(1)}, bf16[96,2048]{1,0:T(8,128)(2,1)S(1)}, u32[]{:S(2)}, u32[]{:S(2)}) %collective-permute-start.23) | collective-permute-done | bytes 393248 | tf_op jit(solution)/shard_map/ppermute | solution.py:250
  200.3 0.9 fusion.20
  201.2 1.5 copy-done
  202.6 3.8 %unpack.1 = (bf16[160,2048]{1,0:T(8,128)(2,1)}, bf16[160,2048]{1,0:T(8,128)(2,1)}) custom-call(s32[160,1]{1,0:T(8,128)} %copy.12.exp_ref, bf16[256,5120]{1,0:T(8,128)(2,1)} %bitcast.114), custom_call_target="tpu_custom_call" | custom-call | tf_op jit(solution)/shard_map/unpack/pallas_call | solution.py:97
  (28 shorter events, 0.2 us)
Async XLA Ops:
  6.3 41.5 %all-to-all-start = ((bf16[32,8,5120]{2,1,0:T(8,128)(2,1)}), bf16[32,8,5120]{2,1,0:T(8,128)(2,1)S(1)}, u32[]{:S(2)}, u32[]{:S(2)}) async-start(bf16[32,8,5120]{2,1,0:T(8,128)(2,1)} %bitcast.115), calls=%async_computation | async-start | bytes 5242880 | tf_op jit(solution)/shard_map/all_to_all | solution.py:280
  47.7 1.5 copy-start.4
  63.7 35.4 %collective-permute-start.16 = (bf16[48,2048]{1,0:T(8,128)(2,1)}, bf16[48,2048]{1,0:T(8,128)(2,1)}, u32[]{:S(2)}, u32[]{:S(2)}) collective-permute-start(bf16[48,2048]{1,0:T(8,128)(2,1)} %get-tuple-element.27), channel_id=1, source_target_pairs={{0,32},{32,64},{64,96},{96,128},{128,160},{160,192},{192,224},{224... | collective-permute-start | bytes 589832 | tf_op jit(solution)/shard_map/ppermute | solution.py:250
  65.6 36.8 %collective-permute-start.20 = (bf16[48,2048]{1,0:T(8,128)(2,1)}, bf16[48,2048]{1,0:T(8,128)(2,1)}, u32[]{:S(2)}, u32[]{:S(2)}) collective-permute-start(bf16[48,2048]{1,0:T(8,128)(2,1)} %get-tuple-element.29), channel_id=1, source_target_pairs={{0,224},{32,0},{64,32},{96,64},{128,96},{160,128},{192,160},{224,1... | collective-permute-start | bytes 589832 | tf_op jit(solution)/shard_map/ppermute | solution.py:250
  79.9 28.0 %collective-permute-start.12 = (bf16[128,768]{1,0:T(8,128)(2,1)}, bf16[128,768]{1,0:T(8,128)(2,1)}, u32[]{:S(2)}, u32[]{:S(2)}) collective-permute-start(bf16[128,768]{1,0:T(8,128)(2,1)} %get-tuple-element.37), channel_id=1, source_target_pairs={{0,224},{32,0},{64,32},{96,64},{128,96},{160,128},{192,160},{224,1... | collective-permute-start | bytes 589832 | tf_op jit(solution)/shard_map/ppermute | solution.py:250
  81.9 26.2 %collective-permute-start.8 = (bf16[128,768]{1,0:T(8,128)(2,1)}, bf16[128,768]{1,0:T(8,128)(2,1)}, u32[]{:S(2)}, u32[]{:S(2)}) collective-permute-start(bf16[128,768]{1,0:T(8,128)(2,1)} %get-tuple-element.35), channel_id=1, source_target_pairs={{0,32},{32,64},{64,96},{96,128},{128,160},{160,192},{192,224},{224... | collective-permute-start | bytes 589832 | tf_op jit(solution)/shard_map/ppermute | solution.py:250
  83.9 25.7 %collective-permute-start = (bf16[128,768]{1,0:T(8,128)(2,1)}, bf16[128,768]{1,0:T(8,128)(2,1)}, u32[]{:S(2)}, u32[]{:S(2)}) collective-permute-start(bf16[128,768]{1,0:T(8,128)(2,1)} %get-tuple-element.43), channel_id=1, source_target_pairs={{0,32},{32,64},{64,96},{96,128},{128,160},{160,192},{192,224},{224... | collective-permute-start | bytes 589832 | tf_op jit(solution)/shard_map/ppermute | solution.py:250
  92.9 108.3 %all-to-all-start.1 = ((bf16[32,8,5120]{2,1,0:T(8,128)(2,1)}), bf16[32,8,5120]{2,1,0:T(8,128)(2,1)S(1)}, u32[]{:S(2)}, u32[]{:S(2)}) async-start(bf16[32,8,5120]{2,1,0:T(8,128)(2,1)} %bitcast.113), calls=%async_computation.1 | async-start | bytes 5242880 | tf_op jit(solution)/shard_map/all_to_all | solution.py:280
  99.1 10.6 %copy-start.2 = (bf16[8,256,768]{2,1,0:T(8,128)(2,1)S(1)}, bf16[8,256,768]{2,1,0:T(8,128)(2,1)}, u32[]{:S(2)}) copy-start(bf16[8,256,768]{2,1,0:T(8,128)(2,1)} %get-tuple-element.20) | copy-start | bytes 9437188
  99.1 10.6 %collective-permute-start.4 = (bf16[128,768]{1,0:T(8,128)(2,1)}, bf16[128,768]{1,0:T(8,128)(2,1)S(1)}, u32[]{:S(2)}, u32[]{:S(2)}) collective-permute-start(bf16[128,768]{1,0:T(8,128)(2,1)} %get-tuple-element.45), channel_id=1, source_target_pairs={{0,224},{32,0},{64,32},{96,64},{128,96},{160,128},{192,160},{224,1... | collective-permute-start | bytes 589832 | tf_op jit(solution)/shard_map/ppermute | solution.py:250
  104.7 54.1 %collective-permute-start.21 = (bf16[96,2048]{1,0:T(8,128)(2,1)S(1)}, bf16[96,2048]{1,0:T(8,128)(2,1)S(1)}, u32[]{:S(2)}, u32[]{:S(2)}) collective-permute-start(bf16[96,2048]{1,0:T(8,128)(2,1)S(1)} %pad_maximum_fusion.5), channel_id=1, source_target_pairs={{0,224},{32,0},{64,32},{96,64},{128,96},{160,128},{192,160},{224,1... | collective-permute-start | bytes 1179656 | tf_op jit(solution)/shard_map/ppermute | solution.py:250
  106.8 23.1 %copy-start.3 = (bf16[8,256,768]{2,1,0:T(8,128)(2,1)S(1)}, bf16[8,256,768]{2,1,0:T(8,128)(2,1)}, u32[]{:S(2)}) copy-start(bf16[8,256,768]{2,1,0:T(8,128)(2,1)} %get-tuple-element.21) | copy-start | bytes 9437188
  107.9 29.0 %collective-permute-start.17 = (bf16[96,2048]{1,0:T(8,128)(2,1)S(1)}, bf16[96,2048]{1,0:T(8,128)(2,1)S(1)}, u32[]{:S(2)}, u32[]{:S(2)}) collective-permute-start(bf16[96,2048]{1,0:T(8,128)(2,1)S(1)} %pad_maximum_fusion.4), channel_id=1, source_target_pairs={{0,32},{32,64},{64,96},{96,128},{128,160},{160,192},{192,224},{224... | collective-permute-start | bytes 1179656 | tf_op jit(solution)/shard_map/ppermute | solution.py:250
  109.5 27.5 %copy-start.1 = (bf16[768,2048]{1,0:T(8,128)(2,1)S(1)}, bf16[768,2048]{1,0:T(8,128)(2,1)}, u32[]{:S(2)}) copy-start(bf16[768,2048]{1,0:T(8,128)(2,1)} %get-tuple-element.22) | copy-start | bytes 9437188
  109.5 20.3 %collective-permute-start.9 = (bf16[256,768]{1,0:T(8,128)(2,1)S(1)}, bf16[256,768]{1,0:T(8,128)(2,1)S(1)}, u32[]{:S(2)}, u32[]{:S(2)}) collective-permute-start(bf16[256,768]{1,0:T(8,128)(2,1)S(1)} %pad_maximum_fusion.2), channel_id=1, source_target_pairs={{0,32},{32,64},{64,96},{96,128},{128,160},{160,192},{192,224},{224... | collective-permute-start | bytes 1179656 | tf_op jit(solution)/shard_map/ppermute | solution.py:250
  110.9 25.9 %collective-permute-start.1 = (bf16[256,768]{1,0:T(8,128)(2,1)S(1)}, bf16[256,768]{1,0:T(8,128)(2,1)S(1)}, u32[]{:S(2)}, u32[]{:S(2)}) collective-permute-start(bf16[256,768]{1,0:T(8,128)(2,1)S(1)} %pad_maximum_fusion), channel_id=1, source_target_pairs={{0,32},{32,64},{64,96},{96,128},{128,160},{160,192},{192,224},{224... | collective-permute-start | bytes 1179656 | tf_op jit(solution)/shard_map/ppermute | solution.py:250
  112.0 25.2 %collective-permute-start.13 = (bf16[256,768]{1,0:T(8,128)(2,1)S(1)}, bf16[256,768]{1,0:T(8,128)(2,1)S(1)}, u32[]{:S(2)}, u32[]{:S(2)}) collective-permute-start(bf16[256,768]{1,0:T(8,128)(2,1)S(1)} %pad_maximum_fusion.3), channel_id=1, source_target_pairs={{0,224},{32,0},{64,32},{96,64},{128,96},{160,128},{192,160},{224,1... | collective-permute-start | bytes 1179656 | tf_op jit(solution)/shard_map/ppermute | solution.py:250
  129.8 20.5 %collective-permute-start.5 = (bf16[256,768]{1,0:T(8,128)(2,1)S(1)}, bf16[256,768]{1,0:T(8,128)(2,1)S(1)}, u32[]{:S(2)}, u32[]{:S(2)}) collective-permute-start(bf16[256,768]{1,0:T(8,128)(2,1)S(1)} %pad_maximum_fusion.1), channel_id=1, source_target_pairs={{0,224},{32,0},{64,32},{96,64},{128,96},{160,128},{192,160},{224,1... | collective-permute-start | bytes 1179656 | tf_op jit(solution)/shard_map/ppermute | solution.py:250
  136.8 13.3 %collective-permute-start.10 = (bf16[256,768]{1,0:T(8,128)(2,1)S(1)}, bf16[256,768]{1,0:T(8,128)(2,1)S(1)}, u32[]{:S(2)}, u32[]{:S(2)}) collective-permute-start(bf16[256,768]{1,0:T(8,128)(2,1)S(1)} %fusion.8), channel_id=1, source_target_pairs={{0,32},{32,64},{64,96},{96,128},{128,160},{160,192},{192,224},{224... | collective-permute-start | bytes 1179656 | tf_op jit(solution)/shard_map/ppermute | solution.py:250
  136.9 21.6 %collective-permute-start.2 = (bf16[256,768]{1,0:T(8,128)(2,1)S(1)}, bf16[256,768]{1,0:T(8,128)(2,1)S(1)}, u32[]{:S(2)}, u32[]{:S(2)}) collective-permute-start(bf16[256,768]{1,0:T(8,128)(2,1)S(1)} %fusion.14), channel_id=1, source_target_pairs={{0,32},{32,64},{64,96},{96,128},{128,160},{160,192},{192,224},{224... | collective-permute-start | bytes 1179656 | tf_op jit(solution)/shard_map/ppermute | solution.py:250
  137.2 27.4 %collective-permute-start.18 = (bf16[96,2048]{1,0:T(8,128)(2,1)S(1)}, bf16[96,2048]{1,0:T(8,128)(2,1)S(1)}, u32[]{:S(2)}, u32[]{:S(2)}) collective-permute-start(bf16[96,2048]{1,0:T(8,128)(2,1)S(1)} %fusion.2), channel_id=1, source_target_pairs={{0,32},{32,64},{64,96},{96,128},{128,160},{160,192},{192,224},{224... | collective-permute-start | bytes 1179656 | tf_op jit(solution)/shard_map/ppermute | solution.py:250
  150.3 16.7 %collective-permute-start.14 = (bf16[256,768]{1,0:T(8,128)(2,1)S(1)}, bf16[256,768]{1,0:T(8,128)(2,1)S(1)}, u32[]{:S(2)}, u32[]{:S(2)}) collective-permute-start(bf16[256,768]{1,0:T(8,128)(2,1)S(1)} %get-tuple-element.32), channel_id=1, source_target_pairs={{0,224},{32,0},{64,32},{96,64},{128,96},{160,128},{192,160},{224,1... | collective-permute-start | bytes 1179656 | tf_op jit(solution)/shard_map/ppermute | solution.py:250
  158.7 9.0 %collective-permute-start.6 = (bf16[256,768]{1,0:T(8,128)(2,1)S(1)}, bf16[256,768]{1,0:T(8,128)(2,1)S(1)}, u32[]{:S(2)}, u32[]{:S(2)}) collective-permute-start(bf16[256,768]{1,0:T(8,128)(2,1)S(1)} %get-tuple-element.40), channel_id=1, source_target_pairs={{0,224},{32,0},{64,32},{96,64},{128,96},{160,128},{192,160},{224,1... | collective-permute-start | bytes 1179656 | tf_op jit(solution)/shard_map/ppermute | solution.py:250
  164.9 12.1 %collective-permute-start.22 = (bf16[96,2048]{1,0:T(8,128)(2,1)S(1)}, bf16[96,2048]{1,0:T(8,128)(2,1)S(1)}, u32[]{:S(2)}, u32[]{:S(2)}) collective-permute-start(bf16[96,2048]{1,0:T(8,128)(2,1)S(1)} %get-tuple-element.24), channel_id=1, source_target_pairs={{0,224},{32,0},{64,32},{96,64},{128,96},{160,128},{192,160},{224,1... | collective-permute-start | bytes 1179656 | tf_op jit(solution)/shard_map/ppermute | solution.py:250
  165.0 29.8 %collective-permute-start.19 = (bf16[96,2048]{1,0:T(8,128)(2,1)S(1)}, bf16[96,2048]{1,0:T(8,128)(2,1)S(1)}, u32[]{:S(2)}, u32[]{:S(2)}) collective-permute-start(bf16[96,2048]{1,0:T(8,128)(2,1)S(1)} %get-tuple-element.23), channel_id=1, source_target_pairs={{0,32},{32,64},{64,96},{96,128},{128,160},{160,192},{192,224},{224... | collective-permute-start | bytes 1179656 | tf_op jit(solution)/shard_map/ppermute | solution.py:250
  167.0 19.8 %collective-permute-start.11 = (bf16[256,768]{1,0:T(8,128)(2,1)S(1)}, bf16[256,768]{1,0:T(8,128)(2,1)S(1)}, u32[]{:S(2)}, u32[]{:S(2)}) collective-permute-start(bf16[256,768]{1,0:T(8,128)(2,1)S(1)} %get-tuple-element.31), channel_id=1, source_target_pairs={{0,32},{32,64},{64,96},{96,128},{128,160},{160,192},{192,224},{224... | collective-permute-start | bytes 1179656 | tf_op jit(solution)/shard_map/ppermute | solution.py:250
  167.0 24.9 %collective-permute-start.3 = (bf16[256,768]{1,0:T(8,128)(2,1)S(1)}, bf16[256,768]{1,0:T(8,128)(2,1)S(1)}, u32[]{:S(2)}, u32[]{:S(2)}) collective-permute-start(bf16[256,768]{1,0:T(8,128)(2,1)S(1)} %get-tuple-element.39), channel_id=1, source_target_pairs={{0,32},{32,64},{64,96},{96,128},{128,160},{160,192},{192,224},{224... | collective-permute-start | bytes 1179656 | tf_op jit(solution)/shard_map/ppermute | solution.py:250
  167.7 19.0 %collective-permute-start.15 = (bf16[256,768]{1,0:T(8,128)(2,1)S(1)}, bf16[256,768]{1,0:T(8,128)(2,1)S(1)}, u32[]{:S(2)}, u32[]{:S(2)}) collective-permute-start(bf16[256,768]{1,0:T(8,128)(2,1)S(1)} %fusion.7), channel_id=1, source_target_pairs={{0,224},{32,0},{64,32},{96,64},{128,96},{160,128},{192,160},{224,1... | collective-permute-start | bytes 1179656 | tf_op jit(solution)/shard_map/ppermute | solution.py:250
  177.0 16.9 %collective-permute-start.7 = (bf16[256,768]{1,0:T(8,128)(2,1)S(1)}, bf16[256,768]{1,0:T(8,128)(2,1)S(1)}, u32[]{:S(2)}, u32[]{:S(2)}) collective-permute-start(bf16[256,768]{1,0:T(8,128)(2,1)S(1)} %fusion.13), channel_id=1, source_target_pairs={{0,224},{32,0},{64,32},{96,64},{128,96},{160,128},{192,160},{224,1... | collective-permute-start | bytes 1179656 | tf_op jit(solution)/shard_map/ppermute | solution.py:250
  186.7 13.5 %collective-permute-start.23 = (bf16[96,2048]{1,0:T(8,128)(2,1)S(1)}, bf16[96,2048]{1,0:T(8,128)(2,1)S(1)}, u32[]{:S(2)}, u32[]{:S(2)}) collective-permute-start(bf16[96,2048]{1,0:T(8,128)(2,1)S(1)} %fusion.1), channel_id=1, source_target_pairs={{0,224},{32,0},{64,32},{96,64},{128,96},{160,128},{192,160},{224,1... | collective-permute-start | bytes 1179656 | tf_op jit(solution)/shard_map/ppermute | solution.py:250
  201.2 1.5 copy-start

commit v2 on v0

v2 whole, which is shorter than its diff:
```python
import functools

import jax
import jax.numpy as jnp
from jax import lax
from jax.experimental import pallas as pl
from jax.experimental.pallas import tpu as pltpu
from jax.sharding import PartitionSpec as P

F32 = jnp.float32
BF16 = jnp.bfloat16
MAIN = 8
QUARTERS = 4
LANES = 256
MIB = 1024 * 1024
FREE = pl.CostEstimate(flops=0, bytes_accessed=0, transcendentals=0)


def mm(a, b, dims):
    return lax.dot_general(a, b, (dims, ((), ())), preferred_element_type=F32)


NN = ((1,), (0,))
NT = ((1,), (1,))
TN = ((0,), (0,))


def params(mib):
    return pltpu.CompilerParams(vmem_limit_bytes=mib * MIB)


def iota(shape, dim):
    return lax.broadcasted_iota(jnp.int32, shape, dim)


def as_col(row):
    tall = jnp.broadcast_to(row.astype(F32), (128, row.shape[1]))
    return jnp.transpose(tall)[:, 0:1].astype(jnp.int32)


def in_hbm(x):
    return pltpu.with_memory_space_constraint(x, pltpu.HBM)


def mask(cond):
    return jnp.where(cond, 1.0, 0.0).astype(BF16)


def pack_kernel(rows, peers, exp_hbm, tok_hbm, gout_hbm, out_hbm, exp_ref, src, out, sem_exp, sem_in, sem_out):
    expert = pltpu.make_async_copy(exp_hbm, exp_ref, sem_exp)
    expert.start()
    width = tok_hbm.shape[1]
    part = width // QUARTERS
    both = width + part
    loads = []
    for k, hbm in enumerate((tok_hbm, gout_hbm)):
        for q in range(QUARTERS):
            cols = pl.ds(q * part, part)
            copy = pltpu.make_async_copy(hbm.at[:, cols], src.at[k, :, cols], sem_in.at[k * QUARTERS + q])
            copy.start()
            loads.append(copy)
    expert.wait()
    row = exp_ref[...]
    earlier = (as_col(row) == row) & (iota((rows, rows), 0) < iota((rows, rows), 1))
    rank = jnp.sum(jnp.where(earlier, 1.0, 0.0), axis=0, keepdims=True).astype(jnp.int32)
    slots = peers * MAIN
    r = iota((slots, rows), 0)
    here = (r >> 3) == row
    whole = mask(here & ((r & 7) == rank))
    late = here & (((r >> 2) & 1) + MAIN == rank)
    late = [mask(late & ((r & 3) == q)) for q in range(QUARTERS)]
    stores = []

    def store(lo, size):
        cols = pl.ds(lo, size)
        copy = pltpu.make_async_copy(out.at[:, cols], out_hbm.at[:, cols], sem_out.at[len(stores)])
        copy.start()
        stores.append(copy)

    for k in range(2):
        at = k * both
        tail = jnp.zeros((slots, part), F32)
        for q in range(QUARTERS):
            loads[k * QUARTERS + q].wait()
            cols = src[k, :, q * part : (q + 1) * part]
            out[:, at + q * part : at + (q + 1) * part] = mm(whole, cols, NN).astype(BF16)
            store(at + q * part, part)
            tail += mm(late[q], cols, NN)
        out[:, at + width : at + both] = tail.astype(BF16)
        store(at + width, part)
    for copy in stores:
        copy.wait()


def pack(expert_row, tokens, grad_out, peers):
    rows, width = tokens.shape
    both = width + width // QUARTERS
    slots = peers * MAIN
    hbm = pl.BlockSpec(memory_space=pltpu.HBM)
    return pl.pallas_call(
        functools.partial(pack_kernel, rows, peers),
        in_specs=[hbm, hbm, hbm],
        out_specs=hbm,
        out_shape=pltpu.HBM((slots, 2 * both), BF16),
        scratch_shapes=[
            pltpu.VMEM((1, rows), jnp.int32),
            pltpu.VMEM((2, rows, width), BF16),
            pltpu.VMEM((slots, 2 * both), BF16),
            pltpu.SemaphoreType.DMA,
            pltpu.SemaphoreType.DMA((2 * QUARTERS,)),
            pltpu.SemaphoreType.DMA((2 * QUARTERS + 2,)),
        ],
        compiler_params=params(12),
        cost_estimate=FREE,
        name="pack",
    )(in_hbm(expert_row), in_hbm(tokens), in_hbm(grad_out))


def fetch_kernel(src, dst, sem):
    copy = pltpu.make_async_copy(src, dst, sem)
    copy.start()
    copy.wait()


def fetch(array):
    return pl.pallas_call(
        fetch_kernel,
        in_specs=[pl.BlockSpec(memory_space=pltpu.HBM)],
        out_specs=pl.BlockSpec(memory_space=pltpu.VMEM),
        out_shape=pltpu.VMEM(array.shape, array.dtype),
        scratch_shapes=[pltpu.SemaphoreType.DMA],
        compiler_params=params(2),
        cost_estimate=FREE,
        name="fetch",
    )(in_hbm(array))


def unpack_kernel(rows, peers, exp_ref, back_ref, mixed_ref, gtok_ref):
    row = exp_ref[...]
    col = as_col(row)
    earlier = (col == row) & (iota((rows, rows), 1) < iota((rows, rows), 0))
    rank = jnp.sum(jnp.where(earlier, 1.0, 0.0), axis=1, keepdims=True).astype(jnp.int32)
    slots = peers * MAIN
    r = iota((rows, slots), 1)
    here = (r >> 3) == col
    whole = mask(here & ((r & 7) == rank))
    late = here & (((r >> 2) & 1) + MAIN == rank)
    part = mixed_ref.shape[1] // QUARTERS
    both = part * (QUARTERS + 1)
    for k, dst in enumerate((mixed_ref, gtok_ref)):
        at = k * both
        tail = back_ref[:, at + QUARTERS * part : at + both]
        for q in range(QUARTERS):
            got = mm(whole, back_ref[:, at + q * part : at + (q + 1) * part], NN)
            got += mm(mask(late & ((r & 3) == q)), tail, NN)
            dst[:, q * part : (q + 1) * part] = got.astype(BF16)


def unpack(expert_row, back, width, peers):
    rows = expert_row.shape[1]
    out = jax.ShapeDtypeStruct((rows, width), BF16)
    return pl.pallas_call(
        functools.partial(unpack_kernel, rows, peers),
        out_shape=(out, out),
        compiler_params=params(12),
        cost_estimate=FREE,
        name="unpack",
    )(expert_row, back)


def grad_block(groups, scale, z, x_ref, dy_ref, cut_ref, gg_ref, gu_ref, a_ref, b_ref):
    rows = x_ref.shape[1] // groups
    half = rows // 2
    at = z % groups
    x = x_ref[:, pl.ds(pl.multiple_of(at * rows, 128), rows)]

    def put(ref, base, value):
        n = value.shape[0]
        for c in range(value.shape[1] // LANES):
            ref[base + c * n : base + (c + 1) * n, :] = value[:, c * LANES : (c + 1) * LANES]
        return base + n * (value.shape[1] // LANES)

    if a_ref is not None and b_ref is not None:
        up = (mm(x, gu_ref[...], TN) * scale).astype(BF16)
        upper, lower = up[:half], up[half:]
    elif a_ref is not None:
        upper = (mm(x[:, :half], gu_ref[...], TN) * scale).astype(BF16)
    else:
        lower = (mm(x[:, half:], gu_ref[...], TN) * scale).astype(BF16)
    if a_ref is not None:
        down = (mm(cut_ref[at], dy_ref[...], TN) * scale).astype(BF16)
        put(a_ref, put(a_ref, 0, down), upper)
    if b_ref is not None:
        gate = (mm(x, gg_ref[...], TN) * scale).astype(BF16)
        put(b_ref, put(b_ref, 0, gate), lower)


def hidden_kernel(
    groups, tile, scale, z_ref, recv_hbm, wg_ref, wu_hbm, wd_hbm,
    x_ref, dy_ref, act_ref, cut_ref, gg_ref, gu_ref, a4, b4, b3, a5,
    recv_ref, wu_ref, wd_ref, gate_ref, up_ref, sem_x, sem_dy, sem_u, sem_d,
):
    slots = recv_ref.shape[0]
    width, inner = wg_ref.shape
    part = width // QUARTERS
    both = width + part
    tails = slots // QUARTERS
    tiles = [slice(lo, lo + tile) for lo in range(0, inner, tile)]
    halves = [(slice(None), slice(0, both)), (slice(None), slice(both, 2 * both))]
    load_x = pltpu.make_async_copy(recv_hbm.at[halves[0]], recv_ref.at[halves[0]], sem_x)
    load_dy = pltpu.make_async_copy(recv_hbm.at[halves[1]], recv_ref.at[halves[1]], sem_dy)
    load_u = pltpu.make_async_copy(wu_hbm, wu_ref, sem_u)
    load_d = pltpu.make_async_copy(wd_hbm, wd_ref, sem_d)
    load_x.start()
    load_u.start()
    load_dy.start()
    load_d.start()
    picks = [
        mask(iota((tails, slots), 1) == iota((tails, slots), 0) * QUARTERS + q) for q in range(QUARTERS)
    ]

    def spread(k, dst):
        at = k * both
        dst[0:slots, :] = recv_ref[:, at : at + width]
        tail = recv_ref[:, at + width : at + both]
        for q in range(QUARTERS):
            dst[slots : slots + tails, q * part : (q + 1) * part] = mm(picks[q], tail, NN).astype(BF16)

    load_x.wait()
    spread(0, x_ref)
    for cols in tiles:
        gate_ref[:, cols] = mm(x_ref[...], wg_ref[:, cols], NN)
    load_u.wait()
    for cols in tiles:
        up_ref[:, cols] = mm(x_ref[...], wu_ref[:, cols], NN)
    load_dy.wait()
    spread(1, dy_ref)
    load_d.wait()
    for cols in tiles:
        gate, up = gate_ref[:, cols], up_ref[:, cols]
        grad_act = mm(dy_ref[...], wd_ref[cols, :], NT)
        sig = jax.nn.sigmoid(gate)
        swish = gate * sig
        act_ref[:, cols] = (swish * up).astype(BF16)
        gg_ref[:, cols] = (grad_act * up * sig * (1.0 + gate * (1.0 - sig))).astype(BF16)
        gu_ref[:, cols] = (grad_act * swish).astype(BF16)
    each = inner // groups
    for k in range(groups):
        cut_ref[k] = act_ref[:, k * each : (k + 1) * each]
    far = groups // 2
    for d, a_ref, b_ref in ((far, a4, b4), (far - 1, None, b3), (far + 1, a5, None)):
        grad_block(groups, scale, z_ref[0] + d, x_ref, dy_ref, cut_ref, gg_ref, gu_ref, a_ref, b_ref)


def hidden(z, recv, wg, wu, wd, scale, groups, tile=256):
    slots = recv.shape[0]
    width, inner = wg.shape
    total = slots + slots // QUARTERS
    shapes = [(total, width)] * 2 + [(total, inner), (groups, total, inner // groups)] + [(total, inner)] * 2
    shapes += [(3 * width * inner // (2 * groups * LANES), LANES)] * 4
    vmem = pl.BlockSpec(memory_space=pltpu.VMEM)
    hbm = pl.BlockSpec(memory_space=pltpu.HBM)
    return pl.pallas_call(
        functools.partial(hidden_kernel, groups, tile, scale),
        in_specs=[pl.BlockSpec(memory_space=pltpu.SMEM), hbm, vmem, hbm, hbm],
        out_specs=[vmem] * len(shapes),
        out_shape=[jax.ShapeDtypeStruct(s, BF16) for s in shapes],
        scratch_shapes=[
            pltpu.VMEM(recv.shape, BF16),
            pltpu.VMEM(wu.shape, BF16),
            pltpu.VMEM(wd.shape, BF16),
            pltpu.VMEM((total, inner), F32),
            pltpu.VMEM((total, inner), F32),
        ]
        + [pltpu.SemaphoreType.DMA] * 4,
        compiler_params=params(24),
        cost_estimate=pl.CostEstimate(
            flops=6 * total * width * inner, bytes_accessed=8 * width * inner, transcendentals=total * inner
        ),
        name="hidden",
    )(z, in_hbm(recv), wg, in_hbm(wu), in_hbm(wd))


def near_kernel(groups, scale, z_ref, cut_ref, x_ref, dy_ref, gg_ref, gu_ref, *refs):
    count = groups - 1
    outs, (a_ref, b_ref, sems) = refs[: 2 * (count - 1)], refs[2 * (count - 1) :]
    copies = []
    for i in range(count):
        z = z_ref[0] + groups // 2 + 1 + i
        a = a_ref.at[i] if i > 0 else None
        b = b_ref.at[i] if i < count - 1 else None
        grad_block(groups, scale, z, x_ref, dy_ref, cut_ref, gg_ref, gu_ref, a, b)
        for ref, out in ((a, i - 1), (b, count - 1 + i)):
            if ref is not None:
                copies.append(pltpu.make_async_copy(ref, outs[out], sems.at[len(copies)]))
                copies[-1].start()
    for copy in copies:
        copy.wait()


def near_blocks(z, cut, x, dy, gg, gu, scale):
    groups, total, each = cut.shape
    width = x.shape[1]
    inner = gg.shape[1]
    vmem = pl.BlockSpec(memory_space=pltpu.VMEM)
    hbm = pl.BlockSpec(memory_space=pltpu.HBM)
    one = (3 * width * inner // (2 * groups * LANES), LANES)
    count = 2 * (groups - 2)
    outs = pl.pallas_call(
        functools.partial(near_kernel, groups, scale),
        in_specs=[pl.BlockSpec(memory_space=pltpu.SMEM)] + [vmem] * 5,
        out_specs=[hbm] * count,
        out_shape=[pltpu.HBM(one, BF16)] * count,
        scratch_shapes=[pltpu.VMEM((groups - 1, *one), BF16)] * 2 + [pltpu.SemaphoreType.DMA((count,))],
        compiler_params=params(16),
        cost_estimate=pl.CostEstimate(
            flops=6 * total * width * inner, bytes_accessed=6 * width * inner, transcendentals=0
        ),
        name="near_blocks",
    )(z, cut, x, dy, gg, gu)
    far = groups // 2
    a = {d: outs[d + far - 2] for d in range(2 - far, far)}
    b = {d: outs[groups - 2 + d + far - 1] for d in range(1 - far, far - 1)}
    return a, b


def almost_kernel(own_a, own_b, al_any, br_any, pa, pb, oa, ob, al, br, sems):
    pairs = ((own_a, oa), (al_any, al), (own_b, ob), (br_any, br))
    loads = [pltpu.make_async_copy(src, dst, sems.at[n]) for n, (src, dst) in enumerate(pairs)]
    for copy in loads:
        copy.start()
    for copy in loads:
        copy.wait()
    pa[...] = oa[...].astype(F32) + al[...].astype(F32)
    pb[...] = ob[...].astype(F32) + br[...].astype(F32)


def almost(own_a, own_b, al, br):
    vmem = pl.BlockSpec(memory_space=pltpu.VMEM)
    return pl.pallas_call(
        almost_kernel,
        in_specs=[pl.BlockSpec(memory_space=pl.ANY)] * 4,
        out_specs=[vmem] * 2,
        out_shape=[pltpu.VMEM(al.shape, F32)] * 2,
        scratch_shapes=[pltpu.VMEM(al.shape, BF16)] * 4 + [pltpu.SemaphoreType.DMA((4,))],
        compiler_params=params(6),
        cost_estimate=FREE,
        name="almost",
    )(in_hbm(own_a), in_hbm(own_b), al, br)


def finish_kernel(after, pa, pb, ar_any, bl_any, down_hbm, gate_hbm, up_hbm, ar, bl, down, gate, up, sem_in, sem_out):
    loads = [
        pltpu.make_async_copy(src, dst, sem_in.at[n]) for n, (src, dst) in enumerate(((ar_any, ar), (bl_any, bl)))
    ]
    for copy in loads:
        copy.start()
    half = up.shape[0] // 2
    stores = []

    def take(part, moved, base, dst):
        rows = dst.shape[0]
        for c in range(dst.shape[1] // LANES):
            at = slice(base + c * rows, base + (c + 1) * rows)
            dst[:, c * LANES : (c + 1) * LANES] = (part[at, :] + moved[at, :].astype(F32)).astype(BF16)
        return base + rows * (dst.shape[1] // LANES)

    def store(src, dst):
        stores.append(pltpu.make_async_copy(src, dst, sem_out.at[len(stores)]))
        stores[-1].start()

    loads[0].wait()
    base = take(pa, ar, 0, down)
    store(down, down_hbm)
    take(pa, ar, base, up.at[:half])
    store(up.at[:half], up_hbm.at[:half])
    loads[1].wait()
    base = take(pb, bl, 0, gate)
    store(gate, gate_hbm)
    take(pb, bl, base, up.at[half:])
    store(up.at[half:], up_hbm.at[half:])
    for copy in stores:
        copy.wait()


def finish(after, sums, ar, bl, groups, width, inner):
    vmem = pl.BlockSpec(memory_space=pltpu.VMEM)
    hbm = pl.BlockSpec(memory_space=pltpu.HBM)
    anywhere = pl.BlockSpec(memory_space=pl.ANY)
    shapes = [(inner // groups, width), (width // groups, inner), (width // groups, inner)]
    return pl.pallas_call(
        finish_kernel,
        in_specs=[anywhere, vmem, vmem, anywhere, anywhere],
        out_specs=[hbm] * 3,
        out_shape=[pltpu.HBM(s, BF16) for s in shapes],
        scratch_shapes=[pltpu.VMEM(ar.shape, BF16)] * 2
        + [pltpu.VMEM(s, BF16) for s in shapes]
        + [pltpu.SemaphoreType.DMA((2,)), pltpu.SemaphoreType.DMA((4,))],
        compiler_params=params(6),
        cost_estimate=FREE,
        name="finish",
    )(in_hbm(after), *sums, ar, bl)


def rows_kernel(
    after, act_ref, gg_ref, gu_ref, wg_hbm, wu_hbm, wd_hbm, out_hbm, wg_ref, wu_ref, wd_ref, out, sem_in, sem_out
):
    slots = out.shape[0]
    width = wg_ref.shape[0]
    part = width // QUARTERS
    both = width + part
    tails = slots // QUARTERS
    loads = []
    for q in range(QUARTERS):
        cut = slice(q * part, (q + 1) * part)
        where = ((wd_hbm, wd_ref, (slice(None), cut)), (wg_hbm, wg_ref, (cut,)), (wu_hbm, wu_ref, (cut,)))
        for n, (src, dst, at) in enumerate(where):
            copy = pltpu.make_async_copy(src.at[at], dst.at[at], sem_in.at[q * 3 + n])
            copy.start()
            loads.append(copy)
    stores = []

    def store(lo):
        cols = pl.ds(lo, part)
        copy = pltpu.make_async_copy(out.at[:, cols], out_hbm.at[:, cols], sem_out.at[len(stores)])
        copy.start()
        stores.append(copy)

    tail = [jnp.zeros((slots, part), F32) for _ in range(2)]
    for q in range(QUARTERS):
        cut = slice(q * part, (q + 1) * part)
        pick = mask(iota((slots, tails), 0) == iota((slots, tails), 1) * QUARTERS + q)
        for k in range(2):
            if k == 0:
                loads[q * 3].wait()
                val = mm(act_ref[...], wd_ref[:, cut], NN).astype(BF16)
            else:
                loads[q * 3 + 1].wait()
                loads[q * 3 + 2].wait()
                val = (mm(gg_ref[...], wg_ref[cut, :], NT) + mm(gu_ref[...], wu_ref[cut, :], NT)).astype(BF16)
            lo = k * both + q * part
            out[:, lo : lo + part] = val[0:slots, :]
            store(lo)
            tail[k] += mm(pick, val[slots : slots + tails, :], NN)
    for k in range(2):
        lo = k * both + width
        out[:, lo : lo + part] = tail[k].astype(BF16)
        store(lo)
    for copy in stores:
        copy.wait()


def rows_back(after, act, gg, gu, wg, wu, wd):
    total, inner = act.shape
    width = wg.shape[0]
    slots = total * QUARTERS // (QUARTERS + 1)
    out = (slots, 2 * (width + width // QUARTERS))
    vmem = pl.BlockSpec(memory_space=pltpu.VMEM)
    hbm = pl.BlockSpec(memory_space=pltpu.HBM)
    return pl.pallas_call(
        rows_kernel,
        in_specs=[pl.BlockSpec(memory_space=pl.ANY), vmem, vmem, vmem, hbm, hbm, hbm],
        out_specs=hbm,
        out_shape=pltpu.HBM(out, BF16),
        scratch_shapes=[
            pltpu.VMEM(wg.shape, BF16),
            pltpu.VMEM(wu.shape, BF16),
            pltpu.VMEM(wd.shape, BF16),
            pltpu.VMEM(out, BF16),
            pltpu.SemaphoreType.DMA((3 * QUARTERS,)),
            pltpu.SemaphoreType.DMA((2 * QUARTERS + 2,)),
        ],
        compiler_params=params(20),
        cost_estimate=pl.CostEstimate(
            flops=6 * total * width * inner, bytes_accessed=6 * width * inner, transcendentals=0
        ),
        name="rows_back",
    )(in_hbm(after), act, gg, gu, in_hbm(wg), in_hbm(wu), in_hbm(wd))


def step_kernel(after, own_r, own_l, r_any, l_any, out_r, out_l, o_r, o_l, r, l, sems):
    pairs = ((own_r, o_r), (r_any, r), (own_l, o_l), (l_any, l))
    loads = [pltpu.make_async_copy(src, dst, sems.at[n]) for n, (src, dst) in enumerate(pairs)]
    for copy in loads:
        copy.start()
    stores = []
    for n, (own, moved, out) in enumerate(((o_r, r, out_r), (o_l, l, out_l))):
        for copy in loads[2 * n : 2 * n + 2]:
            copy.wait()
        own[...] = (own[...].astype(F32) + moved[...].astype(F32)).astype(BF16)
        stores.append(pltpu.make_async_copy(own, out, sems.at[4 + n]))
        stores[n].start()
    for copy in stores:
        copy.wait()


def ring_step(after, own_r, own_l, r, l):
    hbm = pl.BlockSpec(memory_space=pltpu.HBM)
    return pl.pallas_call(
        step_kernel,
        in_specs=[pl.BlockSpec(memory_space=pl.ANY)] * 5,
        out_specs=[hbm] * 2,
        out_shape=[pltpu.HBM(r.shape, BF16)] * 2,
        scratch_shapes=[pltpu.VMEM(r.shape, BF16)] * 4 + [pltpu.SemaphoreType.DMA((6,))],
        compiler_params=params(6),
        cost_estimate=FREE,
        name="ring_step",
    )(in_hbm(after), in_hbm(own_r), in_hbm(own_l), r, l)


def ring_sums(first, rest, groups):
    right = [(i, (i + 1) % groups) for i in range(groups)]
    left = [(i, (i - 1) % groups) for i in range(groups)]
    far = groups // 2
    send = lambda r, l: (lax.ppermute(r, "dp", right), lax.ppermute(l, "dp", left))
    a4, b4, b3, a5 = first
    a, b = 0, 1
    moving = [send(a4, b4), send(b3, a5)]
    after = None
    for n in range(2, 2 * far - 1):
        i, j = (a, b) if n % 2 == 0 else (b, a)
        d = far - (n + 1) // 2
        r, l = moving[n - 2]
        after = ring_step(rest[a][0] if after is None else after[0], rest[i][d], rest[j][-d], r, l)
        moving.append(send(*after))
    br, al = moving[-2]
    return almost(rest[a][0], rest[b][0], al, br), *moving[-1]


def shards(tokens, expert_of, w_gate, w_up, w_down, grad_out):
    rows, width = tokens.shape
    peers = lax.axis_size("expert")
    groups = lax.axis_size("dp")
    wg, wu, wd = w_gate[0], w_up[0], w_down[0]
    scale = float(rows * groups) ** (-0.5)

    def exchange(packed):
        swapped = lax.all_to_all(
            packed.reshape(peers, MAIN, -1), "expert", split_axis=0, concat_axis=0, tiled=True
        )
        return swapped.reshape(peers * MAIN, -1)

    expert_row = expert_of.reshape(1, rows)
    z = lax.axis_index("dp").astype(jnp.int32).reshape(1)
    recv = exchange(pack(expert_row, tokens, grad_out, peers))
    x, dy, act, cut, gg, gu, *first = hidden(z, recv, fetch(wg), wu, wd, scale, groups)
    rest = near_blocks(z, cut, x, dy, gg, gu, scale)
    back = exchange(rows_back(rest[0][0], act, gg, gu, wg, wu, wd))
    sums, ar, bl = ring_sums(first, rest, groups)
    mixed, grad_tokens = unpack(expert_row, back, width, peers)
    grad_down, grad_gate, grad_up = finish(mixed, sums, ar, bl, groups, width, wg.shape[1])
    return mixed, grad_tokens, grad_gate[None], grad_up[None], grad_down[None]


def solution(mesh):
    in_specs = (
        P(("dp", "expert"), None),
        P(("dp", "expert"), None),
        P("expert", None, None),
        P("expert", None, None),
        P("expert", None, None),
        P(("dp", "expert"), None),
    )
    out_specs = (
        P(("dp", "expert"), None),
        P(("dp", "expert"), None),
        P("expert", "dp", None),
        P("expert", "dp", None),
        P("expert", "dp", None),
    )
    return jax.shard_map(shards, mesh=mesh, in_specs=in_specs, out_specs=out_specs, check_vma=False)
```

time: 316 us -> 173 us (0.55)
  waiting for transfers between devices: 183 us -> 83.9 us
  Pallas kernels: 0 us -> 44.5 us
  matrix products: 43.1 us -> 0 us
  local copies, waits for them, and re-layouts: 38.4 us -> 2.07 us
  between operations: 14.2 us -> 1.18 us
  starting transfers between devices: 28 us -> 40.4 us
  other arithmetic: 7.3 us -> 0 us
    reduce_scatter x2 -> x0, waiting for transfers between devices: 99.5 us -> none  [the longest x1 99.5 us: shards(): lax.psum_scatter(jnp.einsum('sr,sf->rf', columns, both_grads, preferred_e...]
    ppermute x0 -> x14, waiting for transfers between devices: none -> 51.9 us  [the longest x7 26.5 us: ring_sums(): lax.ppermute(l, 'dp', left)]
    all_to_all x4 -> x2, waiting for transfers between devices: 83.1 us -> 32 us  [exchange(): lax.all_to_all(packed.reshape(peers, MAIN, -1), 'expert', split_axis=0, c...]
    pallas_call x0 -> x13, Pallas kernels: none -> 44.5 us  [the longest x5 11.5 us: ring_step(): pl.pallas_call(step_kernel, in_specs=[pl.BlockSpec(memory_space=pl.ANY)]...]
    dot_general x12 -> x0, matrix products: 43.1 us -> none  [the longest x1 6.63 us: shards(): jnp.einsum('sr,sf->rf', columns, both_grads, preferred_element_type=jnp.f...]
    reshape x9 -> x0, local copies, waits for them, and re-layouts: 29.3 us -> none  [the longest x1 3.64 us: shards(): arriving = arriving.reshape(peers * slots, width)]
    ppermute x0 -> x14, starting transfers between devices: none -> 26.6 us  [the longest x7 24.4 us: ring_sums(): lax.ppermute(l, 'dp', left)]
    all_to_all x4 -> x2, starting transfers between devices: 27.8 us -> 13.8 us  [exchange(): lax.all_to_all(packed.reshape(peers, MAIN, -1), 'expert', split_axis=0, c...]
  transfers between devices with their start and end apart: 6 -> 16, of which waited for: 5 -> 12; matrix products, arithmetic and copies ran while one was open for 22% -> 0% of each run, Pallas kernels for 0% -> 10%
where the time goes in v2:
time: 173 us; the launch traced here: 172 us
  waiting for transfers between devices  83.9 us (48%)
  Pallas kernels  44.5 us (26%)
  starting transfers between devices  40.4 us (23%)
  local copies, waits for them, and re-layouts  2.07 us (1%)
    all_to_all x2, waiting for transfers between devices, exchange(): lax.all_to_all(packed.reshape(peers, MAIN, -1), 'expert', split_axis=0, c...  32 us
    ppermute x7, waiting for transfers between devices, ring_sums(): lax.ppermute(l, 'dp', left)  26.5 us
    ppermute x7, waiting for transfers between devices, ring_sums(): lax.ppermute(r, 'dp', right)  25.4 us
    ppermute x7, starting transfers between devices, ring_sums(): lax.ppermute(l, 'dp', left)  24.4 us
    all_to_all x2, starting transfers between devices, exchange(): lax.all_to_all(packed.reshape(peers, MAIN, -1), 'expert', split_axis=0, c...  13.8 us
    pallas_call x5, Pallas kernels, ring_step(): pl.pallas_call(step_kernel, in_specs=[pl.BlockSpec(memory_space=pl.ANY)]...  11.5 us
    pallas_call x1, Pallas kernels, hidden(): pl.pallas_call(functools.partial(hidden_kernel, groups, tile, scale), in_...  8.29 us
    pallas_call x1, Pallas kernels, rows_back(): pl.pallas_call(rows_kernel, in_specs=[pl.BlockSpec(memory_space=pl.ANY),...  7.5 us
  transfers between devices with their start and end apart: 16, of which 12 were waited for; matrix products, arithmetic and copies ran while one was open for 0% of the time, Pallas kernels for 10%

profile of v2, /device:TPU:2, one launch (start us, length us, event | category | flops | bytes accessed | tf_op | source)
XLA Modules:
  0.0 172.0 jit_solution(991447363235401302)
XLA Ops:
  0.6 4.3 %pack.1 = bf16[256,5120]{1,0:T(8,128)(2,1)} custom-call(s32[1,160]{1,0:T(1,128)} %bitcast.13, bf16[160,2048]{1,0:T(8,128)(2,1)} %tok_hbm.1, bf16[160,2048]{1,0:T(8,128)(2,1)} %gout_hbm.1), custom_call_target="tpu_custom_call" | custom-call | tf_op jit(solution)/shard_map/pack/pallas_call | solution.py:100
  5.0 7.7 %all-to-all-start = ((bf16[32,8,5120]{2,1,0:T(8,128)(2,1)}), bf16[32,8,5120]{2,1,0:T(8,128)(2,1)}, u32[]{:S(2)}, u32[]{:S(2)}) async-start(bf16[32,8,5120]{2,1,0:T(8,128)(2,1)} %bitcast.22), calls=%async_computation | async-start | bytes 5242880 | tf_op jit(solution)/shard_map/all_to_all | solution.py:538
  12.7 1.9 %fetch.1.wg_ref = bf16[2048,768]{1,0:T(8,128)(2,1)S(1)} custom-call(bf16[2048,768]{1,0:T(8,128)(2,1)} %bitcast.15), custom_call_target="tpu_custom_call" | custom-call | tf_op jit(solution)/shard_map/fetch/pallas_call | solution.py:126
  14.6 32.0 %all-to-all-done = bf16[32,8,5120]{2,1,0:T(8,128)(2,1)} async-done(((bf16[32,8,5120]{2,1,0:T(8,128)(2,1)}), bf16[32,8,5120]{2,1,0:T(8,128)(2,1)}, u32[]{:S(2)}, u32[]{:S(2)}) %all-to-all-start) | async-done | bytes 2621472 | tf_op jit(solution)/shard_map/all_to_all | solution.py:538
  46.6 8.3 %hidden.1 = (bf16[320,2048]{1,0:T(8,128)(2,1)S(1)}, bf16[320,2048]{1,0:T(8,128)(2,1)S(1)}, bf16[320,768]{1,0:T(8,128)(2,1)S(1)}, bf16[8,320,96]{2,1,0:T(8,128)(2...) custom-call(s32[1]{0:T(128)} %bitcast.1.z_ref, ...), custom_call_target="tpu_custom_call" | custom-call | flops 3019898880 | bytes 12582912 | tf_op jit(solution)/shard_map/hidden/pallas_call | solution.py:263
  54.9 0.0 copy-start.5
  54.9 0.0 copy-start.7
  54.9 0.0 copy-start.8
  54.9 0.0 copy-start.9
  54.9 5.1 %near_blocks.1 = (bf16[1152,256]{1,0:T(8,128)(2,1)}, bf16[1152,256]{1,0:T(8,128)(2,1)}, bf16[1152,256]{1,0:T(8,128)(2,1)}, bf16[1152,256]{1,0:T(8,128)(2,1)}, bf...) custom-call(s32[1]{0:T(128)} %bitcast.1.z_ref, ...), custom_call_target="tpu_custom_call" | custom-call | flops 3019898880 | bytes 9437184 | tf_op jit(solution)/shard_map/near_blocks/pallas_call | solution.py:309
  60.0 0.0 copy-done.5
  60.0 7.5 %rows_back.1 = bf16[256,5120]{1,0:T(8,128)(2,1)} custom-call(bf16[1152,256]{1,0:T(8,128)(2,1)} %get-tuple-element.49.after.own_a, bf16[320,768]{1,0:T(8,128)(2,1)S(1)} %get-tuple-element.50.act_ref, bf16[320,768]{1,0:T(8,128)(2,1)S(1)} %get-tuple-element.47.gg_ref, bf16[320,768]{1,0:T(8,128)(2,1)S(1)} %get-tuple-element.48.gu_ref, ...), custom_call_target="tpu_custom_call" | custom-call | flops 3019898880 | bytes 9437184 | tf_op jit(solution)/shard_map/rows_back/pallas_call | solution.py:460
  67.5 0.0 copy-done.7
  67.5 0.0 copy-done.8
  67.6 0.0 copy-done.9
  67.6 0.0 copy-start.6
  67.8 6.2 %all-to-all-start.1 = ((bf16[32,8,5120]{2,1,0:T(8,128)(2,1)}), bf16[32,8,5120]{2,1,0:T(8,128)(2,1)S(1)}, u32[]{:S(2)}, u32[]{:S(2)}) async-start(bf16[32,8,5120]{2,1,0:T(8,128)(2,1)} %bitcast.21), calls=%async_computation.1 | async-start | bytes 5242880 | tf_op jit(solution)/shard_map/all_to_all | solution.py:538
  73.9 2.0 %collective-permute-start = (bf16[1152,256]{1,0:T(8,128)(2,1)}, bf16[1152,256]{1,0:T(8,128)(2,1)S(1)}, u32[]{:S(2)}, u32[]{:S(2)}) collective-permute-start(bf16[1152,256]{1,0:T(8,128)(2,1)} %copy-done.9), channel_id=1, source_target_pairs={{0,32},{32,64},{64,96},{96,128},{128,160},{160,192},{192,224},{224... | collective-permute-start | bytes 1769480 | tf_op jit(solution)/shard_map/ppermute | solution.py:515
  75.9 4.0 %collective-permute-start.1 = (bf16[1152,256]{1,0:T(8,128)(2,1)}, bf16[1152,256]{1,0:T(8,128)(2,1)S(1)}, u32[]{:S(2)}, u32[]{:S(2)}) collective-permute-start(bf16[1152,256]{1,0:T(8,128)(2,1)} %copy-done.8), channel_id=1, source_target_pairs={{0,224},{32,0},{64,32},{96,64},{128,96},{160,128},{192,160},{224,1... | collective-permute-start | bytes 1769480 | tf_op jit(solution)/shard_map/ppermute | solution.py:515
  80.0 0.0 collective-permute-start.2
  80.0 0.0 copy-done.6
  80.0 3.2 %collective-permute-start.3 = (bf16[1152,256]{1,0:T(8,128)(2,1)S(1)}, bf16[1152,256]{1,0:T(8,128)(2,1)S(1)}, u32[]{:S(2)}, u32[]{:S(2)}) collective-permute-start(bf16[1152,256]{1,0:T(8,128)(2,1)S(1)} %copy-done.6), channel_id=1, source_target_pairs={{0,224},{32,0},{64,32},{96,64},{128,96},{160,128},{192,160},{224,1... | collective-permute-start | bytes 1769480 | tf_op jit(solution)/shard_map/ppermute | solution.py:515
  83.2 11.0 %collective-permute-done.r_any = bf16[1152,256]{1,0:T(8,128)(2,1)S(1)} collective-permute-done((bf16[1152,256]{1,0:T(8,128)(2,1)}, bf16[1152,256]{1,0:T(8,128)(2,1)S(1)}, u32[]{:S(2)}, u32[]{:S(2)}) %collective-permute-start) | collective-permute-done | bytes 589856 | tf_op jit(solution)/shard_map/ppermute | solution.py:515
  94.2 0.0 collective-permute-done.1.l_any
  94.2 2.3 %ring_step.5 = (bf16[1152,256]{1,0:T(8,128)(2,1)}, bf16[1152,256]{1,0:T(8,128)(2,1)}) custom-call(bf16[1152,256]{1,0:T(8,128)(2,1)} %get-tuple-element.49.after.own_a, bf16[1152,256]{1,0:T(8,128)(2,1)} %get-tuple-element.54.own_r, bf16[1152,256]{1,0:T(8,128)(2,1)} %get-tuple-element.55.own_l, bf16[1152,256]{1,0:T(8,128)(2,1)S(1)} %collective-permute-done.r_any, ...), custom_call_target="tpu_custom_call" | custom-call | tf_op jit(solution)/shard_map/ring_step/pallas_call | solution.py:499
  96.5 3.4 %collective-permute-start.5 = (bf16[1152,256]{1,0:T(8,128)(2,1)}, bf16[1152,256]{1,0:T(8,128)(2,1)S(1)}, u32[]{:S(2)}, u32[]{:S(2)}) collective-permute-start(bf16[1152,256]{1,0:T(8,128)(2,1)} %get-tuple-element.66), channel_id=1, source_target_pairs={{0,224},{32,0},{64,32},{96,64},{128,96},{160,128},{192,160},{224,1... | collective-permute-start | bytes 1769480 | tf_op jit(solution)/shard_map/ppermute | solution.py:515
  99.9 0.0 collective-permute-start.4
  99.9 6.9 %collective-permute-done.2.r_any = bf16[1152,256]{1,0:T(8,128)(2,1)S(1)} collective-permute-done((bf16[1152,256]{1,0:T(8,128)(2,1)}, bf16[1152,256]{1,0:T(8,128)(2,1)S(1)}, u32[]{:S(2)}, u32[]{:S(2)}) %collective-permute-start.2) | collective-permute-done | bytes 589856 | tf_op jit(solution)/shard_map/ppermute | solution.py:515
  106.8 0.0 collective-permute-done.3.l_any
  106.8 2.3 %ring_step.6 = (bf16[1152,256]{1,0:T(8,128)(2,1)}, bf16[1152,256]{1,0:T(8,128)(2,1)}) custom-call(bf16[1152,256]{1,0:T(8,128)(2,1)} %get-tuple-element.58.after, bf16[1152,256]{1,0:T(8,128)(2,1)} %get-tuple-element.59.own_r, bf16[1152,256]{1,0:T(8,128)(2,1)} %get-tuple-element.60.own_l, bf16[1152,256]{1,0:T(8,128)(2,1)S(1)} %collective-permute-done.2.r_any, ...), custom_call_target="tpu_custom_call" | custom-call | tf_op jit(solution)/shard_map/ring_step/pallas_call | solution.py:499
  109.2 3.4 %collective-permute-start.7 = (bf16[1152,256]{1,0:T(8,128)(2,1)}, bf16[1152,256]{1,0:T(8,128)(2,1)S(1)}, u32[]{:S(2)}, u32[]{:S(2)}) collective-permute-start(bf16[1152,256]{1,0:T(8,128)(2,1)} %get-tuple-element.70), channel_id=1, source_target_pairs={{0,224},{32,0},{64,32},{96,64},{128,96},{160,128},{192,160},{224,1... | collective-permute-start | bytes 1769480 | tf_op jit(solution)/shard_map/ppermute | solution.py:515
  112.6 0.0 collective-permute-start.6
  112.6 6.7 %collective-permute-done.5.l_any = bf16[1152,256]{1,0:T(8,128)(2,1)S(1)} collective-permute-done((bf16[1152,256]{1,0:T(8,128)(2,1)}, bf16[1152,256]{1,0:T(8,128)(2,1)S(1)}, u32[]{:S(2)}, u32[]{:S(2)}) %collective-permute-start.5) | collective-permute-done | bytes 589856 | tf_op jit(solution)/shard_map/ppermute | solution.py:515
  119.3 0.2 collective-permute-done.4.r_any
  119.5 2.3 %ring_step.7 = (bf16[1152,256]{1,0:T(8,128)(2,1)}, bf16[1152,256]{1,0:T(8,128)(2,1)}) custom-call(bf16[1152,256]{1,0:T(8,128)(2,1)} %get-tuple-element.63.after, bf16[1152,256]{1,0:T(8,128)(2,1)} %get-tuple-element.64.own_r, bf16[1152,256]{1,0:T(8,128)(2,1)} %get-tuple-element.65.own_l, bf16[1152,256]{1,0:T(8,128)(2,1)S(1)} %collective-permute-done.4.r_any, ...), custom_call_target="tpu_custom_call" | custom-call | tf_op jit(solution)/shard_map/ring_step/pallas_call | solution.py:499
  121.8 3.4 %collective-permute-start.11 = (bf16[1152,256]{1,0:T(8,128)(2,1)}, bf16[1152,256]{1,0:T(8,128)(2,1)S(1)}, u32[]{:S(2)}, u32[]{:S(2)}) collective-permute-start(bf16[1152,256]{1,0:T(8,128)(2,1)} %get-tuple-element.77), channel_id=1, source_target_pairs={{0,224},{32,0},{64,32},{96,64},{128,96},{160,128},{192,160},{224,1... | collective-permute-start | bytes 1769480 | tf_op jit(solution)/shard_map/ppermute | solution.py:515
  125.2 0.0 collective-permute-start.10
  125.2 6.7 %collective-permute-done.7.l_any = bf16[1152,256]{1,0:T(8,128)(2,1)S(1)} collective-permute-done((bf16[1152,256]{1,0:T(8,128)(2,1)}, bf16[1152,256]{1,0:T(8,128)(2,1)S(1)}, u32[]{:S(2)}, u32[]{:S(2)}) %collective-permute-start.7) | collective-permute-done | bytes 589856 | tf_op jit(solution)/shard_map/ppermute | solution.py:515
  131.9 0.2 collective-permute-done.6.r_any
  132.1 2.3 %ring_step.8 = (bf16[1152,256]{1,0:T(8,128)(2,1)}, bf16[1152,256]{1,0:T(8,128)(2,1)}) custom-call(bf16[1152,256]{1,0:T(8,128)(2,1)} %get-tuple-element.67.after, bf16[1152,256]{1,0:T(8,128)(2,1)} %get-tuple-element.68.own_r, bf16[1152,256]{1,0:T(8,128)(2,1)} %get-tuple-element.69.own_l, bf16[1152,256]{1,0:T(8,128)(2,1)S(1)} %collective-permute-done.6.r_any, ...), custom_call_target="tpu_custom_call" | custom-call | tf_op jit(solution)/shard_map/ring_step/pallas_call | solution.py:499
  134.5 3.4 %collective-permute-start.8 = (bf16[1152,256]{1,0:T(8,128)(2,1)}, bf16[1152,256]{1,0:T(8,128)(2,1)S(1)}, u32[]{:S(2)}, u32[]{:S(2)}) collective-permute-start(bf16[1152,256]{1,0:T(8,128)(2,1)} %get-tuple-element.71), channel_id=1, source_target_pairs={{0,224},{32,0},{64,32},{96,64},{128,96},{160,128},{192,160},{224,1... | collective-permute-start | bytes 1769480 | tf_op jit(solution)/shard_map/ppermute | solution.py:515
  137.9 0.0 collective-permute-start.9
  137.9 6.6 %collective-permute-done.11.l_any = bf16[1152,256]{1,0:T(8,128)(2,1)S(1)} collective-permute-done((bf16[1152,256]{1,0:T(8,128)(2,1)}, bf16[1152,256]{1,0:T(8,128)(2,1)S(1)}, u32[]{:S(2)}, u32[]{:S(2)}) %collective-permute-start.11) | collective-permute-done | bytes 589856 | tf_op jit(solution)/shard_map/ppermute | solution.py:515
  144.5 0.2 collective-permute-done.10.r_any
  144.8 0.0 copy-start.4
  144.8 2.3 %ring_step.9 = (bf16[1152,256]{1,0:T(8,128)(2,1)}, bf16[1152,256]{1,0:T(8,128)(2,1)}) custom-call(bf16[1152,256]{1,0:T(8,128)(2,1)} %get-tuple-element.72.after, bf16[1152,256]{1,0:T(8,128)(2,1)} %get-tuple-element.75.own_r, bf16[1152,256]{1,0:T(8,128)(2,1)} %get-tuple-element.76.own_l, bf16[1152,256]{1,0:T(8,128)(2,1)S(1)} %collective-permute-done.10.r_any, ...), custom_call_target="tpu_custom_call" | custom-call | tf_op jit(solution)/shard_map/ring_step/pallas_call | solution.py:499
  147.1 0.1 collective-permute-start.12
  147.2 3.4 %collective-permute-start.13 = (bf16[1152,256]{1,0:T(8,128)(2,1)}, bf16[1152,256]{1,0:T(8,128)(2,1)}, u32[]{:S(2)}, u32[]{:S(2)}) collective-permute-start(bf16[1152,256]{1,0:T(8,128)(2,1)} %get-tuple-element.79), channel_id=1, source_target_pairs={{0,224},{32,0},{64,32},{96,64},{128,96},{160,128},{192,160},{224,1... | collective-permute-start | bytes 1769480 | tf_op jit(solution)/shard_map/ppermute | solution.py:515
  150.6 6.6 %collective-permute-done.8.al_any = bf16[1152,256]{1,0:T(8,128)(2,1)S(1)} collective-permute-done((bf16[1152,256]{1,0:T(8,128)(2,1)}, bf16[1152,256]{1,0:T(8,128)(2,1)S(1)}, u32[]{:S(2)}, u32[]{:S(2)}) %collective-permute-start.8) | collective-permute-done | bytes 589856 | tf_op jit(solution)/shard_map/ppermute | solution.py:515
  157.2 0.2 collective-permute-done.9.br_any
  157.4 1.5 almost.1
  158.9 0.0 copy-start
  159.0 1.0 copy-done
  160.0 0.0 copy-start.2
  160.0 1.0 copy-done.2
  161.0 0.0 all-to-all-done.1
  161.0 0.0 copy-start.1
  161.0 0.0 copy-done.4
  161.0 2.0 %unpack.1 = (bf16[160,2048]{1,0:T(8,128)(2,1)}, bf16[160,2048]{1,0:T(8,128)(2,1)}) custom-call(s32[1,160]{1,0:T(1,128)S(1)} %bitcast.14, bf16[256,5120]{1,0:T(8,128)(2,1)S(1)} %bitcast.12), custom_call_target="tpu_custom_call" | custom-call | tf_op jit(solution)/shard_map/unpack/pallas_call | solution.py:162
  163.0 6.6 %collective-permute-done.12.ar_any = bf16[1152,256]{1,0:T(8,128)(2,1)S(1)} collective-permute-done((bf16[1152,256]{1,0:T(8,128)(2,1)}, bf16[1152,256]{1,0:T(8,128)(2,1)S(1)}, u32[]{:S(2)}, u32[]{:S(2)}) %collective-permute-start.12) | collective-permute-done | bytes 589856 | tf_op jit(solution)/shard_map/ppermute | solution.py:515
  169.6 0.0 collective-permute-done.13.bl_any
  169.6 0.0 copy-done.1
  169.6 0.0 copy-done.3
  169.6 2.3 %finish.1 = (bf16[96,2048]{1,0:T(8,128)(2,1)}, bf16[256,768]{1,0:T(8,128)(2,1)}, bf16[256,768]{1,0:T(8,128)(2,1)}) custom-call(bf16[160,2048]{1,0:T(8,128)(2,1)} %get-tuple-element.39.after, f32[1152,256]{1,0:T(8,128)S(1)} %copy-done.1, f32[1152,256]{1,0:T(8,128)S(1)} %copy-done.3, bf16[1152,256]{1,0:T(8,128)(2,1)S(1)} %collective-permute-done.12.ar_any, ...), custom_call_target="tpu_custom_call" | custom-call | tf_op jit(solution)/shard_map/finish/pallas_call | solution.py:391
  (1 shorter events, 0.0 us)
Async XLA Ops:
  5.0 41.6 %all-to-all-start = ((bf16[32,8,5120]{2,1,0:T(8,128)(2,1)}), bf16[32,8,5120]{2,1,0:T(8,128)(2,1)}, u32[]{:S(2)}, u32[]{:S(2)}) async-start(bf16[32,8,5120]{2,1,0:T(8,128)(2,1)} %bitcast.22), calls=%async_computation | async-start | bytes 5242880 | tf_op jit(solution)/shard_map/all_to_all | solution.py:538
  54.9 5.2 %copy-start.5 = (bf16[1152,256]{1,0:T(8,128)(2,1)}, bf16[1152,256]{1,0:T(8,128)(2,1)S(1)}, u32[]{:S(2)}) copy-start(bf16[1152,256]{1,0:T(8,128)(2,1)S(1)} %get-tuple-element.62) | copy-start | bytes 1769476
  54.9 12.7 %copy-start.7 = (bf16[1152,256]{1,0:T(8,128)(2,1)}, bf16[1152,256]{1,0:T(8,128)(2,1)S(1)}, u32[]{:S(2)}) copy-start(bf16[1152,256]{1,0:T(8,128)(2,1)S(1)} %get-tuple-element.61) | copy-start | bytes 1769476
  54.9 12.7 %copy-start.8 = (bf16[1152,256]{1,0:T(8,128)(2,1)}, bf16[1152,256]{1,0:T(8,128)(2,1)S(1)}, u32[]{:S(2)}) copy-start(bf16[1152,256]{1,0:T(8,128)(2,1)S(1)} %get-tuple-element.57) | copy-start | bytes 1769476
  54.9 12.7 %copy-start.9 = (bf16[1152,256]{1,0:T(8,128)(2,1)}, bf16[1152,256]{1,0:T(8,128)(2,1)S(1)}, u32[]{:S(2)}) copy-start(bf16[1152,256]{1,0:T(8,128)(2,1)S(1)} %get-tuple-element.56) | copy-start | bytes 1769476
  67.6 12.4 %copy-start.6 = (bf16[1152,256]{1,0:T(8,128)(2,1)S(1)}, bf16[1152,256]{1,0:T(8,128)(2,1)}, u32[]{:S(2)}) copy-start(bf16[1152,256]{1,0:T(8,128)(2,1)} %copy-done.5) | copy-start | bytes 1769476
  67.8 93.2 %all-to-all-start.1 = ((bf16[32,8,5120]{2,1,0:T(8,128)(2,1)}), bf16[32,8,5120]{2,1,0:T(8,128)(2,1)S(1)}, u32[]{:S(2)}, u32[]{:S(2)}) async-start(bf16[32,8,5120]{2,1,0:T(8,128)(2,1)} %bitcast.21), calls=%async_computation.1 | async-start | bytes 5242880 | tf_op jit(solution)/shard_map/all_to_all | solution.py:538
  73.9 20.3 %collective-permute-start = (bf16[1152,256]{1,0:T(8,128)(2,1)}, bf16[1152,256]{1,0:T(8,128)(2,1)S(1)}, u32[]{:S(2)}, u32[]{:S(2)}) collective-permute-start(bf16[1152,256]{1,0:T(8,128)(2,1)} %copy-done.9), channel_id=1, source_target_pairs={{0,32},{32,64},{64,96},{96,128},{128,160},{160,192},{192,224},{224... | collective-permute-start | bytes 1769480 | tf_op jit(solution)/shard_map/ppermute | solution.py:515
  75.9 18.3 %collective-permute-start.1 = (bf16[1152,256]{1,0:T(8,128)(2,1)}, bf16[1152,256]{1,0:T(8,128)(2,1)S(1)}, u32[]{:S(2)}, u32[]{:S(2)}) collective-permute-start(bf16[1152,256]{1,0:T(8,128)(2,1)} %copy-done.8), channel_id=1, source_target_pairs={{0,224},{32,0},{64,32},{96,64},{128,96},{160,128},{192,160},{224,1... | collective-permute-start | bytes 1769480 | tf_op jit(solution)/shard_map/ppermute | solution.py:515
  80.0 26.9 %collective-permute-start.2 = (bf16[1152,256]{1,0:T(8,128)(2,1)}, bf16[1152,256]{1,0:T(8,128)(2,1)S(1)}, u32[]{:S(2)}, u32[]{:S(2)}) collective-permute-start(bf16[1152,256]{1,0:T(8,128)(2,1)} %copy-done.7), channel_id=1, source_target_pairs={{0,32},{32,64},{64,96},{96,128},{128,160},{160,192},{192,224},{224... | collective-permute-start | bytes 1769480 | tf_op jit(solution)/shard_map/ppermute | solution.py:515
  80.0 26.9 %collective-permute-start.3 = (bf16[1152,256]{1,0:T(8,128)(2,1)S(1)}, bf16[1152,256]{1,0:T(8,128)(2,1)S(1)}, u32[]{:S(2)}, u32[]{:S(2)}) collective-permute-start(bf16[1152,256]{1,0:T(8,128)(2,1)S(1)} %copy-done.6), channel_id=1, source_target_pairs={{0,224},{32,0},{64,32},{96,64},{128,96},{160,128},{192,160},{224,1... | collective-permute-start | bytes 1769480 | tf_op jit(solution)/shard_map/ppermute | solution.py:515
  96.5 22.7 %collective-permute-start.5 = (bf16[1152,256]{1,0:T(8,128)(2,1)}, bf16[1152,256]{1,0:T(8,128)(2,1)S(1)}, u32[]{:S(2)}, u32[]{:S(2)}) collective-permute-start(bf16[1152,256]{1,0:T(8,128)(2,1)} %get-tuple-element.66), channel_id=1, source_target_pairs={{0,224},{32,0},{64,32},{96,64},{128,96},{160,128},{192,160},{224,1... | collective-permute-start | bytes 1769480 | tf_op jit(solution)/shard_map/ppermute | solution.py:515
  99.9 19.5 %collective-permute-start.4 = (bf16[1152,256]{1,0:T(8,128)(2,1)}, bf16[1152,256]{1,0:T(8,128)(2,1)S(1)}, u32[]{:S(2)}, u32[]{:S(2)}) collective-permute-start(bf16[1152,256]{1,0:T(8,128)(2,1)} %get-tuple-element.58.after), channel_id=1, source_target_pairs={{0,32},{32,64},{64,96},{96,128},{128,160},{160,192},{192,224},{224... | collective-permute-start | bytes 1769480 | tf_op jit(solution)/shard_map/ppermute | solution.py:515
  109.2 22.7 %collective-permute-start.7 = (bf16[1152,256]{1,0:T(8,128)(2,1)}, bf16[1152,256]{1,0:T(8,128)(2,1)S(1)}, u32[]{:S(2)}, u32[]{:S(2)}) collective-permute-start(bf16[1152,256]{1,0:T(8,128)(2,1)} %get-tuple-element.70), channel_id=1, source_target_pairs={{0,224},{32,0},{64,32},{96,64},{128,96},{160,128},{192,160},{224,1... | collective-permute-start | bytes 1769480 | tf_op jit(solution)/shard_map/ppermute | solution.py:515
  112.6 19.5 %collective-permute-start.6 = (bf16[1152,256]{1,0:T(8,128)(2,1)}, bf16[1152,256]{1,0:T(8,128)(2,1)S(1)}, u32[]{:S(2)}, u32[]{:S(2)}) collective-permute-start(bf16[1152,256]{1,0:T(8,128)(2,1)} %get-tuple-element.63.after), channel_id=1, source_target_pairs={{0,32},{32,64},{64,96},{96,128},{128,160},{160,192},{192,224},{224... | collective-permute-start | bytes 1769480 | tf_op jit(solution)/shard_map/ppermute | solution.py:515
  121.8 22.8 %collective-permute-start.11 = (bf16[1152,256]{1,0:T(8,128)(2,1)}, bf16[1152,256]{1,0:T(8,128)(2,1)S(1)}, u32[]{:S(2)}, u32[]{:S(2)}) collective-permute-start(bf16[1152,256]{1,0:T(8,128)(2,1)} %get-tuple-element.77), channel_id=1, source_target_pairs={{0,224},{32,0},{64,32},{96,64},{128,96},{160,128},{192,160},{224,1... | collective-permute-start | bytes 1769480 | tf_op jit(solution)/shard_map/ppermute | solution.py:515
  125.2 19.5 %collective-permute-start.10 = (bf16[1152,256]{1,0:T(8,128)(2,1)}, bf16[1152,256]{1,0:T(8,128)(2,1)S(1)}, u32[]{:S(2)}, u32[]{:S(2)}) collective-permute-start(bf16[1152,256]{1,0:T(8,128)(2,1)} %get-tuple-element.67.after), channel_id=1, source_target_pairs={{0,32},{32,64},{64,96},{96,128},{128,160},{160,192},{192,224},{224... | collective-permute-start | bytes 1769480 | tf_op jit(solution)/shard_map/ppermute | solution.py:515
  134.5 22.7 %collective-permute-start.8 = (bf16[1152,256]{1,0:T(8,128)(2,1)}, bf16[1152,256]{1,0:T(8,128)(2,1)S(1)}, u32[]{:S(2)}, u32[]{:S(2)}) collective-permute-start(bf16[1152,256]{1,0:T(8,128)(2,1)} %get-tuple-element.71), channel_id=1, source_target_pairs={{0,224},{32,0},{64,32},{96,64},{128,96},{160,128},{192,160},{224,1... | collective-permute-start | bytes 1769480 | tf_op jit(solution)/shard_map/ppermute | solution.py:515
  137.9 19.5 %collective-permute-start.9 = (bf16[1152,256]{1,0:T(8,128)(2,1)}, bf16[1152,256]{1,0:T(8,128)(2,1)S(1)}, u32[]{:S(2)}, u32[]{:S(2)}) collective-permute-start(bf16[1152,256]{1,0:T(8,128)(2,1)} %get-tuple-element.72.after), channel_id=1, source_target_pairs={{0,32},{32,64},{64,96},{96,128},{128,160},{160,192},{192,224},{224... | collective-permute-start | bytes 1769480 | tf_op jit(solution)/shard_map/ppermute | solution.py:515
  144.8 16.2 %copy-start.4 = (s32[160,1]{0,1:T(1,128)S(1)}, s32[160,1]{0,1:T(1,128)}, u32[]{:S(2)}) copy-start(s32[160,1]{0,1:T(1,128)} %param.7) | copy-start | bytes 1924
  147.1 22.5 %collective-permute-start.12 = (bf16[1152,256]{1,0:T(8,128)(2,1)}, bf16[1152,256]{1,0:T(8,128)(2,1)S(1)}, u32[]{:S(2)}, u32[]{:S(2)}) collective-permute-start(bf16[1152,256]{1,0:T(8,128)(2,1)} %get-tuple-element.78), channel_id=1, source_target_pairs={{0,32},{32,64},{64,96},{96,128},{128,160},{160,192},{192,224},{224... | collective-permute-start | bytes 1769480 | tf_op jit(solution)/shard_map/ppermute | solution.py:515
  147.2 22.4 %collective-permute-start.13 = (bf16[1152,256]{1,0:T(8,128)(2,1)}, bf16[1152,256]{1,0:T(8,128)(2,1)}, u32[]{:S(2)}, u32[]{:S(2)}) collective-permute-start(bf16[1152,256]{1,0:T(8,128)(2,1)} %get-tuple-element.79), channel_id=1, source_target_pairs={{0,224},{32,0},{64,32},{96,64},{128,96},{160,128},{192,160},{224,1... | collective-permute-start | bytes 1769480 | tf_op jit(solution)/shard_map/ppermute | solution.py:515
  158.9 1.0 copy-start
  160.0 1.0 copy-start.2
  161.0 8.6 %copy-start.1 = (f32[1152,256]{1,0:T(8,128)S(1)}, f32[1152,256]{1,0:T(8,128)}, u32[]{:S(2)}) copy-start(f32[1152,256]{1,0:T(8,128)} %copy-done) | copy-start | bytes 3538948
  161.0 8.6 %copy-start.3 = (f32[1152,256]{1,0:T(8,128)S(1)}, f32[1152,256]{1,0:T(8,128)}, u32[]{:S(2)}) copy-start(f32[1152,256]{1,0:T(8,128)} %copy-done.2) | copy-start | bytes 3538948

commit v3 on v2

--- a/solution.py
+++ b/solution.py
@@ -197,8 +197,8 @@
 
 def hidden_kernel(
     groups, tile, scale, z_ref, recv_hbm, wg_ref, wu_hbm, wd_hbm,
-    x_ref, dy_ref, act_ref, cut_ref, gg_ref, gu_ref, a4, b4, b3, a5,
-    recv_ref, wu_ref, wd_ref, gate_ref, up_ref, sem_x, sem_dy, sem_u, sem_d,
+    x_ref, dy_ref, act_ref, cut_ref, gg_ref, gu_ref, a4_hbm, b4_hbm, b3_hbm, a5_hbm,
+    recv_ref, wu_ref, wd_ref, gate_ref, up_ref, a4, b4, b3, a5, sem_x, sem_dy, sem_u, sem_d, sem_out,
 ):
     slots = recv_ref.shape[0]
     width, inner = wg_ref.shape
@@ -248,8 +248,22 @@
     for k in range(groups):
         cut_ref[k] = act_ref[:, k * each : (k + 1) * each]
     far = groups // 2
-    for d, a_ref, b_ref in ((far, a4, b4), (far - 1, None, b3), (far + 1, a5, None)):
-        grad_block(groups, scale, z_ref[0] + d, x_ref, dy_ref, cut_ref, gg_ref, gu_ref, a_ref, b_ref)
+    z = z_ref[0]
+    stores = []
+
+    def store(src, dst):
+        stores.append(pltpu.make_async_copy(src, dst, sem_out.at[len(stores)]))
+        stores[-1].start()
+
+    grad_block(groups, scale, z + far, x_ref, dy_ref, cut_ref, gg_ref, gu_ref, a4, b4)
+    store(a4, a4_hbm)
+    store(b4, b4_hbm)
+    grad_block(groups, scale, z + far - 1, x_ref, dy_ref, cut_ref, gg_ref, gu_ref, None, b3)
+    store(b3, b3_hbm)
+    grad_block(groups, scale, z + far + 1, x_ref, dy_ref, cut_ref, gg_ref, gu_ref, a5, None)
+    store(a5, a5_hbm)
+    for copy in stores:
+        copy.wait()
 
 
 def hidden(z, recv, wg, wu, wd, scale, groups, tile=256):
@@ -257,14 +271,14 @@
     width, inner = wg.shape
     total = slots + slots // QUARTERS
     shapes = [(total, width)] * 2 + [(total, inner), (groups, total, inner // groups)] + [(total, inner)] * 2
-    shapes += [(3 * width * inner // (2 * groups * LANES), LANES)] * 4
+    leaving = (3 * width * inner // (2 * groups * LANES), LANES)
     vmem = pl.BlockSpec(memory_space=pltpu.VMEM)
     hbm = pl.BlockSpec(memory_space=pltpu.HBM)
     return pl.pallas_call(
         functools.partial(hidden_kernel, groups, tile, scale),
         in_specs=[pl.BlockSpec(memory_space=pltpu.SMEM), hbm, vmem, hbm, hbm],
-        out_specs=[vmem] * len(shapes),
-        out_shape=[jax.ShapeDtypeStruct(s, BF16) for s in shapes],
+        out_specs=[vmem] * len(shapes) + [hbm] * 4,
+        out_shape=[jax.ShapeDtypeStruct(s, BF16) for s in shapes] + [pltpu.HBM(leaving, BF16)] * 4,
         scratch_shapes=[
             pltpu.VMEM(recv.shape, BF16),
             pltpu.VMEM(wu.shape, BF16),
@@ -272,7 +286,9 @@
             pltpu.VMEM((total, inner), F32),
             pltpu.VMEM((total, inner), F32),
         ]
-        + [pltpu.SemaphoreType.DMA] * 4,
+        + [pltpu.VMEM(leaving, BF16)] * 4
+        + [pltpu.SemaphoreType.DMA] * 4
+        + [pltpu.SemaphoreType.DMA((4,))],
         compiler_params=params(24),
         cost_estimate=pl.CostEstimate(
             flops=6 * total * width * inner, bytes_accessed=8 * width * inner, transcendentals=total * inner
@@ -503,7 +519,7 @@
         out_shape=[pltpu.HBM(r.shape, BF16)] * 2,
         scratch_shapes=[pltpu.VMEM(r.shape, BF16)] * 4 + [pltpu.SemaphoreType.DMA((6,))],
         compiler_params=params(6),
-        cost_estimate=FREE,
+        cost_estimate=pl.CostEstimate(flops=10**10, bytes_accessed=0, transcendentals=0),
         name="ring_step",
     )(in_hbm(after), in_hbm(own_r), in_hbm(own_l), r, l)
 

time: 173 us -> 158 us (0.913)
  waiting for transfers between devices: 83.9 us -> 73.2 us
  starting transfers between devices: 40.4 us -> 34.8 us
    ppermute x7, waiting for transfers between devices: 25.4 us -> 13.8 us  [ring_sums(): lax.ppermute(r, 'dp', right)]
    ppermute x7, starting transfers between devices: 24.4 us -> 13.3 us  [ring_sums(): lax.ppermute(l, 'dp', left)]
    ppermute x7, starting transfers between devices: 2.16 us -> 7.65 us  [ring_sums(): lax.ppermute(r, 'dp', right)]
  transfers between devices with their start and end apart: 16 -> 16, of which waited for: 12 -> 10; matrix products, arithmetic and copies ran while one was open for 0% -> 0% of each run, Pallas kernels for 10% -> 19%
where the time goes in v3:
time: 158 us; the launch traced here: 157 us
  waiting for transfers between devices  73.2 us (46%)
  Pallas kernels  46.1 us (29%)
  starting transfers between devices  34.8 us (22%)
  local copies, waits for them, and re-layouts  2.05 us (1%)
    all_to_all x2, waiting for transfers between devices, exchange(): lax.all_to_all(packed.reshape(peers, MAIN, -1), 'expert', split_axis=0, c...  32 us
    ppermute x7, waiting for transfers between devices, ring_sums(): lax.ppermute(l, 'dp', left)  27.4 us
    all_to_all x2, starting transfers between devices, exchange(): lax.all_to_all(packed.reshape(peers, MAIN, -1), 'expert', split_axis=0, c...  13.9 us
    ppermute x7, waiting for transfers between devices, ring_sums(): lax.ppermute(r, 'dp', right)  13.8 us
    ppermute x7, starting transfers between devices, ring_sums(): lax.ppermute(l, 'dp', left)  13.3 us
    pallas_call x5, Pallas kernels, ring_step(): pl.pallas_call(step_kernel, in_specs=[pl.BlockSpec(memory_space=pl.ANY)]...  12 us
    pallas_call x1, Pallas kernels, hidden(): pl.pallas_call(functools.partial(hidden_kernel, groups, tile, scale), in_...  9.53 us
    ppermute x7, starting transfers between devices, ring_sums(): lax.ppermute(r, 'dp', right)  7.65 us
  transfers between devices with their start and end apart: 16, of which 10 were waited for; matrix products, arithmetic and copies ran while one was open for 0% of the time, Pallas kernels for 19%

profile of v3, /device:TPU:2, one launch (start us, length us, event | category | flops | bytes accessed | tf_op | source)
XLA Modules:
  0.0 157.1 jit_solution(5855268288785757201)
XLA Ops:
  0.6 4.4 %pack.1 = bf16[256,5120]{1,0:T(8,128)(2,1)} custom-call(s32[1,160]{1,0:T(1,128)} %bitcast.13, bf16[160,2048]{1,0:T(8,128)(2,1)} %tok_hbm.1, bf16[160,2048]{1,0:T(8,128)(2,1)} %gout_hbm.1), custom_call_target="tpu_custom_call" | custom-call | tf_op jit(solution)/shard_map/pack/pallas_call | solution.py:100
  5.0 7.7 %all-to-all-start = ((bf16[32,8,5120]{2,1,0:T(8,128)(2,1)}), bf16[32,8,5120]{2,1,0:T(8,128)(2,1)}, u32[]{:S(2)}, u32[]{:S(2)}) async-start(bf16[32,8,5120]{2,1,0:T(8,128)(2,1)} %bitcast.22), calls=%async_computation | async-start | bytes 5242880 | tf_op jit(solution)/shard_map/all_to_all | solution.py:554
  12.7 1.9 %fetch.1.wg_ref = bf16[2048,768]{1,0:T(8,128)(2,1)S(1)} custom-call(bf16[2048,768]{1,0:T(8,128)(2,1)} %bitcast.15), custom_call_target="tpu_custom_call" | custom-call | tf_op jit(solution)/shard_map/fetch/pallas_call | solution.py:126
  14.6 32.0 %all-to-all-done = bf16[32,8,5120]{2,1,0:T(8,128)(2,1)} async-done(((bf16[32,8,5120]{2,1,0:T(8,128)(2,1)}), bf16[32,8,5120]{2,1,0:T(8,128)(2,1)}, u32[]{:S(2)}, u32[]{:S(2)}) %all-to-all-start) | async-done | bytes 2621472 | tf_op jit(solution)/shard_map/all_to_all | solution.py:554
  46.6 9.5 %hidden.1 = (bf16[320,2048]{1,0:T(8,128)(2,1)S(1)}, bf16[320,2048]{1,0:T(8,128)(2,1)S(1)}, bf16[320,768]{1,0:T(8,128)(2,1)S(1)}, bf16[8,320,96]{2,1,0:T(8,128)(2...) custom-call(s32[1]{0:T(128)} %bitcast.1.z_ref, ...), custom_call_target="tpu_custom_call" | custom-call | flops 3019898880 | bytes 12582912 | tf_op jit(solution)/shard_map/hidden/pallas_call | solution.py:277
  56.1 2.0 %collective-permute-start = (bf16[1152,256]{1,0:T(8,128)(2,1)}, bf16[1152,256]{1,0:T(8,128)(2,1)}, u32[]{:S(2)}, u32[]{:S(2)}) collective-permute-start(bf16[1152,256]{1,0:T(8,128)(2,1)} %get-tuple-element.56), channel_id=1, source_target_pairs={{0,32},{32,64},{64,96},{96,128},{128,160},{160,192},{192,224},{224... | collective-permute-start | bytes 1769480 | tf_op jit(solution)/shard_map/ppermute | solution.py:531
  58.1 4.0 %collective-permute-start.1 = (bf16[1152,256]{1,0:T(8,128)(2,1)}, bf16[1152,256]{1,0:T(8,128)(2,1)}, u32[]{:S(2)}, u32[]{:S(2)}) collective-permute-start(bf16[1152,256]{1,0:T(8,128)(2,1)} %get-tuple-element.57), channel_id=1, source_target_pairs={{0,224},{32,0},{64,32},{96,64},{128,96},{160,128},{192,160},{224,1... | collective-permute-start | bytes 1769480 | tf_op jit(solution)/shard_map/ppermute | solution.py:531
  62.1 0.0 collective-permute-start.2
  62.1 3.2 %collective-permute-start.3 = (bf16[1152,256]{1,0:T(8,128)(2,1)}, bf16[1152,256]{1,0:T(8,128)(2,1)}, u32[]{:S(2)}, u32[]{:S(2)}) collective-permute-start(bf16[1152,256]{1,0:T(8,128)(2,1)} %get-tuple-element.62), channel_id=1, source_target_pairs={{0,224},{32,0},{64,32},{96,64},{128,96},{160,128},{192,160},{224,1... | collective-permute-start | bytes 1769480 | tf_op jit(solution)/shard_map/ppermute | solution.py:531
  65.4 5.1 %near_blocks.1 = (bf16[1152,256]{1,0:T(8,128)(2,1)}, bf16[1152,256]{1,0:T(8,128)(2,1)}, bf16[1152,256]{1,0:T(8,128)(2,1)}, bf16[1152,256]{1,0:T(8,128)(2,1)}, bf...) custom-call(s32[1]{0:T(128)} %bitcast.1.z_ref, ...), custom_call_target="tpu_custom_call" | custom-call | flops 3019898880 | bytes 9437184 | tf_op jit(solution)/shard_map/near_blocks/pallas_call | solution.py:325
  70.5 7.5 %rows_back.1 = bf16[256,5120]{1,0:T(8,128)(2,1)} custom-call(bf16[1152,256]{1,0:T(8,128)(2,1)} %get-tuple-element.49.after.own_a, bf16[320,768]{1,0:T(8,128)(2,1)S(1)} %get-tuple-element.50.act_ref, bf16[320,768]{1,0:T(8,128)(2,1)S(1)} %get-tuple-element.47.gg_ref, bf16[320,768]{1,0:T(8,128)(2,1)S(1)} %get-tuple-element.48.gu_ref, ...), custom_call_target="tpu_custom_call" | custom-call | flops 3019898880 | bytes 9437184 | tf_op jit(solution)/shard_map/rows_back/pallas_call | solution.py:476
  78.0 6.2 %all-to-all-start.1 = ((bf16[32,8,5120]{2,1,0:T(8,128)(2,1)}), bf16[32,8,5120]{2,1,0:T(8,128)(2,1)S(1)}, u32[]{:S(2)}, u32[]{:S(2)}) async-start(bf16[32,8,5120]{2,1,0:T(8,128)(2,1)} %bitcast.21), calls=%async_computation.1 | async-start | bytes 5242880 | tf_op jit(solution)/shard_map/all_to_all | solution.py:554
  84.1 0.0 collective-permute-done.r_any
  84.2 0.0 collective-permute-done.1.l_any
  84.2 2.6 %ring_step.5 = (bf16[1152,256]{1,0:T(8,128)(2,1)}, bf16[1152,256]{1,0:T(8,128)(2,1)}) custom-call(bf16[1152,256]{1,0:T(8,128)(2,1)} %get-tuple-element.49.after.own_a, bf16[1152,256]{1,0:T(8,128)(2,1)} %get-tuple-element.54.own_r, bf16[1152,256]{1,0:T(8,128)(2,1)} %get-tuple-element.55.own_l, bf16[1152,256]{1,0:T(8,128)(2,1)} %collective-permute-done.r_any, ...), custom_call_target="tpu_custom_call" | custom-call | flops 10000000000 | tf_op jit(solution)/shard_map/ring_step/pallas_call | solution.py:515
  86.8 0.8 collective-permute-start.5
  87.6 1.3 collective-permute-start.4
  88.9 0.0 collective-permute-done.2.r_any
  88.9 0.0 collective-permute-done.3.l_any
  88.9 2.5 %ring_step.6 = (bf16[1152,256]{1,0:T(8,128)(2,1)}, bf16[1152,256]{1,0:T(8,128)(2,1)}) custom-call(bf16[1152,256]{1,0:T(8,128)(2,1)} %get-tuple-element.58.after, bf16[1152,256]{1,0:T(8,128)(2,1)} %get-tuple-element.59.own_r, bf16[1152,256]{1,0:T(8,128)(2,1)} %get-tuple-element.60.own_l, bf16[1152,256]{1,0:T(8,128)(2,1)S(1)} %collective-permute-done.2.r_any, ...), custom_call_target="tpu_custom_call" | custom-call | flops 10000000000 | tf_op jit(solution)/shard_map/ring_step/pallas_call | solution.py:515
  91.3 2.0 %collective-permute-start.7 = (bf16[1152,256]{1,0:T(8,128)(2,1)}, bf16[1152,256]{1,0:T(8,128)(2,1)S(1)}, u32[]{:S(2)}, u32[]{:S(2)}) collective-permute-start(bf16[1152,256]{1,0:T(8,128)(2,1)} %get-tuple-element.70), channel_id=1, source_target_pairs={{0,224},{32,0},{64,32},{96,64},{128,96},{160,128},{192,160},{224,1... | collective-permute-start | bytes 1769480 | tf_op jit(solution)/shard_map/ppermute | solution.py:531
  93.3 0.1 collective-permute-start.6
  93.5 9.8 %collective-permute-done.5.l_any = bf16[1152,256]{1,0:T(8,128)(2,1)S(1)} collective-permute-done((bf16[1152,256]{1,0:T(8,128)(2,1)}, bf16[1152,256]{1,0:T(8,128)(2,1)S(1)}, u32[]{:S(2)}, u32[]{:S(2)}) %collective-permute-start.5) | collective-permute-done | bytes 589856 | tf_op jit(solution)/shard_map/ppermute | solution.py:531
  103.2 2.0 %collective-permute-done.4.r_any = bf16[1152,256]{1,0:T(8,128)(2,1)S(1)} collective-permute-done((bf16[1152,256]{1,0:T(8,128)(2,1)}, bf16[1152,256]{1,0:T(8,128)(2,1)S(1)}, u32[]{:S(2)}, u32[]{:S(2)}) %collective-permute-start.4) | collective-permute-done | bytes 589856 | tf_op jit(solution)/shard_map/ppermute | solution.py:531
  105.2 2.3 %ring_step.7 = (bf16[1152,256]{1,0:T(8,128)(2,1)}, bf16[1152,256]{1,0:T(8,128)(2,1)}) custom-call(bf16[1152,256]{1,0:T(8,128)(2,1)} %get-tuple-element.63.after, bf16[1152,256]{1,0:T(8,128)(2,1)} %get-tuple-element.64.own_r, bf16[1152,256]{1,0:T(8,128)(2,1)} %get-tuple-element.65.own_l, bf16[1152,256]{1,0:T(8,128)(2,1)S(1)} %collective-permute-done.4.r_any, ...), custom_call_target="tpu_custom_call" | custom-call | flops 10000000000 | tf_op jit(solution)/shard_map/ring_step/pallas_call | solution.py:515
  107.5 0.1 collective-permute-start.11
  107.6 2.0 %collective-permute-start.10 = (bf16[1152,256]{1,0:T(8,128)(2,1)}, bf16[1152,256]{1,0:T(8,128)(2,1)S(1)}, u32[]{:S(2)}, u32[]{:S(2)}) collective-permute-start(bf16[1152,256]{1,0:T(8,128)(2,1)} %get-tuple-element.67.after), channel_id=1, source_target_pairs={{0,32},{32,64},{64,96},{96,128},{128,160},{160,192},{192,224},{224... | collective-permute-start | bytes 1769480 | tf_op jit(solution)/shard_map/ppermute | solution.py:531
  109.6 6.3 %collective-permute-done.7.l_any = bf16[1152,256]{1,0:T(8,128)(2,1)S(1)} collective-permute-done((bf16[1152,256]{1,0:T(8,128)(2,1)}, bf16[1152,256]{1,0:T(8,128)(2,1)S(1)}, u32[]{:S(2)}, u32[]{:S(2)}) %collective-permute-start.7) | collective-permute-done | bytes 589856 | tf_op jit(solution)/shard_map/ppermute | solution.py:531
  115.9 2.0 %collective-permute-done.6.r_any = bf16[1152,256]{1,0:T(8,128)(2,1)S(1)} collective-permute-done((bf16[1152,256]{1,0:T(8,128)(2,1)}, bf16[1152,256]{1,0:T(8,128)(2,1)S(1)}, u32[]{:S(2)}, u32[]{:S(2)}) %collective-permute-start.6) | collective-permute-done | bytes 589856 | tf_op jit(solution)/shard_map/ppermute | solution.py:531
  117.8 2.3 %ring_step.8 = (bf16[1152,256]{1,0:T(8,128)(2,1)}, bf16[1152,256]{1,0:T(8,128)(2,1)}) custom-call(bf16[1152,256]{1,0:T(8,128)(2,1)} %get-tuple-element.67.after, bf16[1152,256]{1,0:T(8,128)(2,1)} %get-tuple-element.68.own_r, bf16[1152,256]{1,0:T(8,128)(2,1)} %get-tuple-element.69.own_l, bf16[1152,256]{1,0:T(8,128)(2,1)S(1)} %collective-permute-done.6.r_any, ...), custom_call_target="tpu_custom_call" | custom-call | flops 10000000000 | tf_op jit(solution)/shard_map/ring_step/pallas_call | solution.py:515
  120.2 0.1 collective-permute-start.8
  120.2 2.0 %collective-permute-start.9 = (bf16[1152,256]{1,0:T(8,128)(2,1)}, bf16[1152,256]{1,0:T(8,128)(2,1)S(1)}, u32[]{:S(2)}, u32[]{:S(2)}) collective-permute-start(bf16[1152,256]{1,0:T(8,128)(2,1)} %get-tuple-element.72.after), channel_id=1, source_target_pairs={{0,32},{32,64},{64,96},{96,128},{128,160},{160,192},{192,224},{224... | collective-permute-start | bytes 1769480 | tf_op jit(solution)/shard_map/ppermute | solution.py:531
  122.3 6.3 %collective-permute-done.11.l_any = bf16[1152,256]{1,0:T(8,128)(2,1)S(1)} collective-permute-done((bf16[1152,256]{1,0:T(8,128)(2,1)}, bf16[1152,256]{1,0:T(8,128)(2,1)S(1)}, u32[]{:S(2)}, u32[]{:S(2)}) %collective-permute-start.11) | collective-permute-done | bytes 589856 | tf_op jit(solution)/shard_map/ppermute | solution.py:531
  128.5 2.0 %collective-permute-done.10.r_any = bf16[1152,256]{1,0:T(8,128)(2,1)S(1)} collective-permute-done((bf16[1152,256]{1,0:T(8,128)(2,1)}, bf16[1152,256]{1,0:T(8,128)(2,1)S(1)}, u32[]{:S(2)}, u32[]{:S(2)}) %collective-permute-start.10) | collective-permute-done | bytes 589856 | tf_op jit(solution)/shard_map/ppermute | solution.py:531
  130.5 0.0 copy-start.4
  130.5 2.3 %ring_step.9 = (bf16[1152,256]{1,0:T(8,128)(2,1)}, bf16[1152,256]{1,0:T(8,128)(2,1)}) custom-call(bf16[1152,256]{1,0:T(8,128)(2,1)} %get-tuple-element.72.after, bf16[1152,256]{1,0:T(8,128)(2,1)} %get-tuple-element.75.own_r, bf16[1152,256]{1,0:T(8,128)(2,1)} %get-tuple-element.76.own_l, bf16[1152,256]{1,0:T(8,128)(2,1)S(1)} %collective-permute-done.10.r_any, ...), custom_call_target="tpu_custom_call" | custom-call | flops 10000000000 | tf_op jit(solution)/shard_map/ring_step/pallas_call | solution.py:515
  132.8 0.2 collective-permute-start.12
  133.0 3.1 %collective-permute-start.13 = (bf16[1152,256]{1,0:T(8,128)(2,1)}, bf16[1152,256]{1,0:T(8,128)(2,1)}, u32[]{:S(2)}, u32[]{:S(2)}) collective-permute-start(bf16[1152,256]{1,0:T(8,128)(2,1)} %get-tuple-element.79), channel_id=1, source_target_pairs={{0,224},{32,0},{64,32},{96,64},{128,96},{160,128},{192,160},{224,1... | collective-permute-start | bytes 1769480 | tf_op jit(solution)/shard_map/ppermute | solution.py:531
  136.1 5.1 %collective-permute-done.8.al_any = bf16[1152,256]{1,0:T(8,128)(2,1)S(1)} collective-permute-done((bf16[1152,256]{1,0:T(8,128)(2,1)}, bf16[1152,256]{1,0:T(8,128)(2,1)S(1)}, u32[]{:S(2)}, u32[]{:S(2)}) %collective-permute-start.8) | collective-permute-done | bytes 589856 | tf_op jit(solution)/shard_map/ppermute | solution.py:531
  141.2 2.0 %collective-permute-done.9.br_any = bf16[1152,256]{1,0:T(8,128)(2,1)S(1)} collective-permute-done((bf16[1152,256]{1,0:T(8,128)(2,1)}, bf16[1152,256]{1,0:T(8,128)(2,1)S(1)}, u32[]{:S(2)}, u32[]{:S(2)}) %collective-permute-start.9) | collective-permute-done | bytes 589856 | tf_op jit(solution)/shard_map/ppermute | solution.py:531
  143.1 1.5 almost.1
  144.7 0.0 copy-start
  144.7 1.0 copy-done
  145.7 0.0 copy-start.2
  145.7 1.0 copy-done.2
  146.7 0.0 all-to-all-done.1
  146.7 0.0 copy-start.1
  146.7 0.0 copy-start.3
  146.7 0.0 copy-done.4
  146.7 2.0 %unpack.1 = (bf16[160,2048]{1,0:T(8,128)(2,1)}, bf16[160,2048]{1,0:T(8,128)(2,1)}) custom-call(s32[1,160]{1,0:T(1,128)S(1)} %bitcast.14, bf16[256,5120]{1,0:T(8,128)(2,1)S(1)} %bitcast.12), custom_call_target="tpu_custom_call" | custom-call | tf_op jit(solution)/shard_map/unpack/pallas_call | solution.py:162
  148.7 6.0 %collective-permute-done.12.ar_any = bf16[1152,256]{1,0:T(8,128)(2,1)S(1)} collective-permute-done((bf16[1152,256]{1,0:T(8,128)(2,1)}, bf16[1152,256]{1,0:T(8,128)(2,1)S(1)}, u32[]{:S(2)}, u32[]{:S(2)}) %collective-permute-start.12) | collective-permute-done | bytes 589856 | tf_op jit(solution)/shard_map/ppermute | solution.py:531
  154.6 0.0 collective-permute-done.13.bl_any
  154.6 0.0 copy-done.1
  154.6 0.0 copy-done.3
  154.7 2.3 %finish.1 = (bf16[96,2048]{1,0:T(8,128)(2,1)}, bf16[256,768]{1,0:T(8,128)(2,1)}, bf16[256,768]{1,0:T(8,128)(2,1)}) custom-call(bf16[160,2048]{1,0:T(8,128)(2,1)} %get-tuple-element.39.after, f32[1152,256]{1,0:T(8,128)S(1)} %copy-done.1, f32[1152,256]{1,0:T(8,128)S(1)} %copy-done.3, bf16[1152,256]{1,0:T(8,128)(2,1)S(1)} %collective-permute-done.12.ar_any, ...), custom_call_target="tpu_custom_call" | custom-call | tf_op jit(solution)/shard_map/finish/pallas_call | solution.py:407
Async XLA Ops:
  5.0 41.6 %all-to-all-start = ((bf16[32,8,5120]{2,1,0:T(8,128)(2,1)}), bf16[32,8,5120]{2,1,0:T(8,128)(2,1)}, u32[]{:S(2)}, u32[]{:S(2)}) async-start(bf16[32,8,5120]{2,1,0:T(8,128)(2,1)} %bitcast.22), calls=%async_computation | async-start | bytes 5242880 | tf_op jit(solution)/shard_map/all_to_all | solution.py:554
  56.1 28.0 %collective-permute-start = (bf16[1152,256]{1,0:T(8,128)(2,1)}, bf16[1152,256]{1,0:T(8,128)(2,1)}, u32[]{:S(2)}, u32[]{:S(2)}) collective-permute-start(bf16[1152,256]{1,0:T(8,128)(2,1)} %get-tuple-element.56), channel_id=1, source_target_pairs={{0,32},{32,64},{64,96},{96,128},{128,160},{160,192},{192,224},{224... | collective-permute-start | bytes 1769480 | tf_op jit(solution)/shard_map/ppermute | solution.py:531
  58.1 26.0 %collective-permute-start.1 = (bf16[1152,256]{1,0:T(8,128)(2,1)}, bf16[1152,256]{1,0:T(8,128)(2,1)}, u32[]{:S(2)}, u32[]{:S(2)}) collective-permute-start(bf16[1152,256]{1,0:T(8,128)(2,1)} %get-tuple-element.57), channel_id=1, source_target_pairs={{0,224},{32,0},{64,32},{96,64},{128,96},{160,128},{192,160},{224,1... | collective-permute-start | bytes 1769480 | tf_op jit(solution)/shard_map/ppermute | solution.py:531
  62.1 26.7 %collective-permute-start.2 = (bf16[1152,256]{1,0:T(8,128)(2,1)}, bf16[1152,256]{1,0:T(8,128)(2,1)S(1)}, u32[]{:S(2)}, u32[]{:S(2)}) collective-permute-start(bf16[1152,256]{1,0:T(8,128)(2,1)} %get-tuple-element.61), channel_id=1, source_target_pairs={{0,32},{32,64},{64,96},{96,128},{128,160},{160,192},{192,224},{224... | collective-permute-start | bytes 1769480 | tf_op jit(solution)/shard_map/ppermute | solution.py:531
  62.1 26.7 %collective-permute-start.3 = (bf16[1152,256]{1,0:T(8,128)(2,1)}, bf16[1152,256]{1,0:T(8,128)(2,1)}, u32[]{:S(2)}, u32[]{:S(2)}) collective-permute-start(bf16[1152,256]{1,0:T(8,128)(2,1)} %get-tuple-element.62), channel_id=1, source_target_pairs={{0,224},{32,0},{64,32},{96,64},{128,96},{160,128},{192,160},{224,1... | collective-permute-start | bytes 1769480 | tf_op jit(solution)/shard_map/ppermute | solution.py:531
  78.0 68.8 %all-to-all-start.1 = ((bf16[32,8,5120]{2,1,0:T(8,128)(2,1)}), bf16[32,8,5120]{2,1,0:T(8,128)(2,1)S(1)}, u32[]{:S(2)}, u32[]{:S(2)}) async-start(bf16[32,8,5120]{2,1,0:T(8,128)(2,1)} %bitcast.21), calls=%async_computation.1 | async-start | bytes 5242880 | tf_op jit(solution)/shard_map/all_to_all | solution.py:554
  86.8 16.5 %collective-permute-start.5 = (bf16[1152,256]{1,0:T(8,128)(2,1)}, bf16[1152,256]{1,0:T(8,128)(2,1)S(1)}, u32[]{:S(2)}, u32[]{:S(2)}) collective-permute-start(bf16[1152,256]{1,0:T(8,128)(2,1)} %get-tuple-element.66), channel_id=1, source_target_pairs={{0,224},{32,0},{64,32},{96,64},{128,96},{160,128},{192,160},{224,1... | collective-permute-start | bytes 1769480 | tf_op jit(solution)/shard_map/ppermute | solution.py:531
  87.6 17.6 %collective-permute-start.4 = (bf16[1152,256]{1,0:T(8,128)(2,1)}, bf16[1152,256]{1,0:T(8,128)(2,1)S(1)}, u32[]{:S(2)}, u32[]{:S(2)}) collective-permute-start(bf16[1152,256]{1,0:T(8,128)(2,1)} %get-tuple-element.58.after), channel_id=1, source_target_pairs={{0,32},{32,64},{64,96},{96,128},{128,160},{160,192},{192,224},{224... | collective-permute-start | bytes 1769480 | tf_op jit(solution)/shard_map/ppermute | solution.py:531
  91.3 24.5 %collective-permute-start.7 = (bf16[1152,256]{1,0:T(8,128)(2,1)}, bf16[1152,256]{1,0:T(8,128)(2,1)S(1)}, u32[]{:S(2)}, u32[]{:S(2)}) collective-permute-start(bf16[1152,256]{1,0:T(8,128)(2,1)} %get-tuple-element.70), channel_id=1, source_target_pairs={{0,224},{32,0},{64,32},{96,64},{128,96},{160,128},{192,160},{224,1... | collective-permute-start | bytes 1769480 | tf_op jit(solution)/shard_map/ppermute | solution.py:531
  93.3 24.5 %collective-permute-start.6 = (bf16[1152,256]{1,0:T(8,128)(2,1)}, bf16[1152,256]{1,0:T(8,128)(2,1)S(1)}, u32[]{:S(2)}, u32[]{:S(2)}) collective-permute-start(bf16[1152,256]{1,0:T(8,128)(2,1)} %get-tuple-element.63.after), channel_id=1, source_target_pairs={{0,32},{32,64},{64,96},{96,128},{128,160},{160,192},{192,224},{224... | collective-permute-start | bytes 1769480 | tf_op jit(solution)/shard_map/ppermute | solution.py:531
  107.5 21.0 %collective-permute-start.11 = (bf16[1152,256]{1,0:T(8,128)(2,1)}, bf16[1152,256]{1,0:T(8,128)(2,1)S(1)}, u32[]{:S(2)}, u32[]{:S(2)}) collective-permute-start(bf16[1152,256]{1,0:T(8,128)(2,1)} %get-tuple-element.77), channel_id=1, source_target_pairs={{0,224},{32,0},{64,32},{96,64},{128,96},{160,128},{192,160},{224,1... | collective-permute-start | bytes 1769480 | tf_op jit(solution)/shard_map/ppermute | solution.py:531
  107.6 22.9 %collective-permute-start.10 = (bf16[1152,256]{1,0:T(8,128)(2,1)}, bf16[1152,256]{1,0:T(8,128)(2,1)S(1)}, u32[]{:S(2)}, u32[]{:S(2)}) collective-permute-start(bf16[1152,256]{1,0:T(8,128)(2,1)} %get-tuple-element.67.after), channel_id=1, source_target_pairs={{0,32},{32,64},{64,96},{96,128},{128,160},{160,192},{192,224},{224... | collective-permute-start | bytes 1769480 | tf_op jit(solution)/shard_map/ppermute | solution.py:531
  120.2 21.0 %collective-permute-start.8 = (bf16[1152,256]{1,0:T(8,128)(2,1)}, bf16[1152,256]{1,0:T(8,128)(2,1)S(1)}, u32[]{:S(2)}, u32[]{:S(2)}) collective-permute-start(bf16[1152,256]{1,0:T(8,128)(2,1)} %get-tuple-element.71), channel_id=1, source_target_pairs={{0,224},{32,0},{64,32},{96,64},{128,96},{160,128},{192,160},{224,1... | collective-permute-start | bytes 1769480 | tf_op jit(solution)/shard_map/ppermute | solution.py:531
  120.2 22.9 %collective-permute-start.9 = (bf16[1152,256]{1,0:T(8,128)(2,1)}, bf16[1152,256]{1,0:T(8,128)(2,1)S(1)}, u32[]{:S(2)}, u32[]{:S(2)}) collective-permute-start(bf16[1152,256]{1,0:T(8,128)(2,1)} %get-tuple-element.72.after), channel_id=1, source_target_pairs={{0,32},{32,64},{64,96},{96,128},{128,160},{160,192},{192,224},{224... | collective-permute-start | bytes 1769480 | tf_op jit(solution)/shard_map/ppermute | solution.py:531
  130.5 16.2 %copy-start.4 = (s32[160,1]{0,1:T(1,128)S(1)}, s32[160,1]{0,1:T(1,128)}, u32[]{:S(2)}) copy-start(s32[160,1]{0,1:T(1,128)} %param.7) | copy-start | bytes 1924
  132.8 21.9 %collective-permute-start.12 = (bf16[1152,256]{1,0:T(8,128)(2,1)}, bf16[1152,256]{1,0:T(8,128)(2,1)S(1)}, u32[]{:S(2)}, u32[]{:S(2)}) collective-permute-start(bf16[1152,256]{1,0:T(8,128)(2,1)} %get-tuple-element.78), channel_id=1, source_target_pairs={{0,32},{32,64},{64,96},{96,128},{128,160},{160,192},{192,224},{224... | collective-permute-start | bytes 1769480 | tf_op jit(solution)/shard_map/ppermute | solution.py:531
  133.0 21.7 %collective-permute-start.13 = (bf16[1152,256]{1,0:T(8,128)(2,1)}, bf16[1152,256]{1,0:T(8,128)(2,1)}, u32[]{:S(2)}, u32[]{:S(2)}) collective-permute-start(bf16[1152,256]{1,0:T(8,128)(2,1)} %get-tuple-element.79), channel_id=1, source_target_pairs={{0,224},{32,0},{64,32},{96,64},{128,96},{160,128},{192,160},{224,1... | collective-permute-start | bytes 1769480 | tf_op jit(solution)/shard_map/ppermute | solution.py:531
  144.7 1.0 copy-start
  145.7 1.0 copy-start.2
  146.7 7.9 %copy-start.1 = (f32[1152,256]{1,0:T(8,128)S(1)}, f32[1152,256]{1,0:T(8,128)}, u32[]{:S(2)}) copy-start(f32[1152,256]{1,0:T(8,128)} %copy-done) | copy-start | bytes 3538948
  146.7 7.9 %copy-start.3 = (f32[1152,256]{1,0:T(8,128)S(1)}, f32[1152,256]{1,0:T(8,128)}, u32[]{:S(2)}) copy-start(f32[1152,256]{1,0:T(8,128)} %copy-done.2) | copy-start | bytes 3538948

commit v4 on v3

--- a/solution.py
+++ b/solution.py
@@ -54,11 +54,9 @@
     both = width + part
     loads = []
     for k, hbm in enumerate((tok_hbm, gout_hbm)):
-        for q in range(QUARTERS):
-            cols = pl.ds(q * part, part)
-            copy = pltpu.make_async_copy(hbm.at[:, cols], src.at[k, :, cols], sem_in.at[k * QUARTERS + q])
-            copy.start()
-            loads.append(copy)
+        copy = pltpu.make_async_copy(hbm, src.at[k], sem_in.at[k])
+        copy.start()
+        loads.append(copy)
     expert.wait()
     row = exp_ref[...]
     earlier = (as_col(row) == row) & (iota((rows, rows), 0) < iota((rows, rows), 1))
@@ -80,8 +78,8 @@
     for k in range(2):
         at = k * both
         tail = jnp.zeros((slots, part), F32)
+        loads[k].wait()
         for q in range(QUARTERS):
-            loads[k * QUARTERS + q].wait()
             cols = src[k, :, q * part : (q + 1) * part]
             out[:, at + q * part : at + (q + 1) * part] = mm(whole, cols, NN).astype(BF16)
             store(at + q * part, part)

time: 158 us -> 157 us (level)
  no operation moved by 1% of the time
where the time goes in v4:
time: 157 us; the launch traced here: 156 us
  waiting for transfers between devices  73.2 us (47%)
  Pallas kernels  45.3 us (29%)
  starting transfers between devices  34.8 us (22%)
  local copies, waits for them, and re-layouts  2.05 us (1%)
    all_to_all x2, waiting for transfers between devices, exchange(): lax.all_to_all(packed.reshape(peers, MAIN, -1), 'expert', split_axis=0, c...  32 us
    ppermute x7, waiting for transfers between devices, ring_sums(): lax.ppermute(l, 'dp', left)  27.4 us
    all_to_all x2, starting transfers between devices, exchange(): lax.all_to_all(packed.reshape(peers, MAIN, -1), 'expert', split_axis=0, c...  13.8 us
    ppermute x7, waiting for transfers between devices, ring_sums(): lax.ppermute(r, 'dp', right)  13.8 us
    ppermute x7, starting transfers between devices, ring_sums(): lax.ppermute(l, 'dp', left)  13.3 us
    pallas_call x5, Pallas kernels, ring_step(): pl.pallas_call(step_kernel, in_specs=[pl.BlockSpec(memory_space=pl.ANY)]...  12 us
    pallas_call x1, Pallas kernels, hidden(): pl.pallas_call(functools.partial(hidden_kernel, groups, tile, scale), in_...  9.54 us
    ppermute x7, starting transfers between devices, ring_sums(): lax.ppermute(r, 'dp', right)  7.64 us
  transfers between devices with their start and end apart: 16, of which 10 were waited for; matrix products, arithmetic and copies ran while one was open for 0% of the time, Pallas kernels for 19%

profile of v4, /device:TPU:2, one launch (start us, length us, event | category | flops | bytes accessed | tf_op | source)
XLA Modules:
  0.0 156.3 jit_solution(16507282158746576751)
XLA Ops:
  0.6 3.5 %pack.1 = bf16[256,5120]{1,0:T(8,128)(2,1)} custom-call(s32[1,160]{1,0:T(1,128)} %bitcast.13, bf16[160,2048]{1,0:T(8,128)(2,1)} %tok_hbm.1, bf16[160,2048]{1,0:T(8,128)(2,1)} %gout_hbm.1), custom_call_target="tpu_custom_call" | custom-call | tf_op jit(solution)/shard_map/pack/pallas_call | solution.py:98
  4.2 7.7 %all-to-all-start = ((bf16[32,8,5120]{2,1,0:T(8,128)(2,1)}), bf16[32,8,5120]{2,1,0:T(8,128)(2,1)}, u32[]{:S(2)}, u32[]{:S(2)}) async-start(bf16[32,8,5120]{2,1,0:T(8,128)(2,1)} %bitcast.22), calls=%async_computation | async-start | bytes 5242880 | tf_op jit(solution)/shard_map/all_to_all | solution.py:552
  11.9 1.9 %fetch.1.wg_ref = bf16[2048,768]{1,0:T(8,128)(2,1)S(1)} custom-call(bf16[2048,768]{1,0:T(8,128)(2,1)} %bitcast.15), custom_call_target="tpu_custom_call" | custom-call | tf_op jit(solution)/shard_map/fetch/pallas_call | solution.py:124
  13.8 32.0 %all-to-all-done = bf16[32,8,5120]{2,1,0:T(8,128)(2,1)} async-done(((bf16[32,8,5120]{2,1,0:T(8,128)(2,1)}), bf16[32,8,5120]{2,1,0:T(8,128)(2,1)}, u32[]{:S(2)}, u32[]{:S(2)}) %all-to-all-start) | async-done | bytes 2621472 | tf_op jit(solution)/shard_map/all_to_all | solution.py:552
  45.7 9.5 %hidden.1 = (bf16[320,2048]{1,0:T(8,128)(2,1)S(1)}, bf16[320,2048]{1,0:T(8,128)(2,1)S(1)}, bf16[320,768]{1,0:T(8,128)(2,1)S(1)}, bf16[8,320,96]{2,1,0:T(8,128)(2...) custom-call(s32[1]{0:T(128)} %bitcast.1.z_ref, ...), custom_call_target="tpu_custom_call" | custom-call | flops 3019898880 | bytes 12582912 | tf_op jit(solution)/shard_map/hidden/pallas_call | solution.py:275
  55.3 2.0 %collective-permute-start = (bf16[1152,256]{1,0:T(8,128)(2,1)}, bf16[1152,256]{1,0:T(8,128)(2,1)}, u32[]{:S(2)}, u32[]{:S(2)}) collective-permute-start(bf16[1152,256]{1,0:T(8,128)(2,1)} %get-tuple-element.56), channel_id=1, source_target_pairs={{0,32},{32,64},{64,96},{96,128},{128,160},{160,192},{192,224},{224... | collective-permute-start | bytes 1769480 | tf_op jit(solution)/shard_map/ppermute | solution.py:529
  57.3 4.0 %collective-permute-start.1 = (bf16[1152,256]{1,0:T(8,128)(2,1)}, bf16[1152,256]{1,0:T(8,128)(2,1)}, u32[]{:S(2)}, u32[]{:S(2)}) collective-permute-start(bf16[1152,256]{1,0:T(8,128)(2,1)} %get-tuple-element.57), channel_id=1, source_target_pairs={{0,224},{32,0},{64,32},{96,64},{128,96},{160,128},{192,160},{224,1... | collective-permute-start | bytes 1769480 | tf_op jit(solution)/shard_map/ppermute | solution.py:529
  61.3 0.0 collective-permute-start.2
  61.3 3.2 %collective-permute-start.3 = (bf16[1152,256]{1,0:T(8,128)(2,1)}, bf16[1152,256]{1,0:T(8,128)(2,1)}, u32[]{:S(2)}, u32[]{:S(2)}) collective-permute-start(bf16[1152,256]{1,0:T(8,128)(2,1)} %get-tuple-element.62), channel_id=1, source_target_pairs={{0,224},{32,0},{64,32},{96,64},{128,96},{160,128},{192,160},{224,1... | collective-permute-start | bytes 1769480 | tf_op jit(solution)/shard_map/ppermute | solution.py:529
  64.5 5.1 %near_blocks.1 = (bf16[1152,256]{1,0:T(8,128)(2,1)}, bf16[1152,256]{1,0:T(8,128)(2,1)}, bf16[1152,256]{1,0:T(8,128)(2,1)}, bf16[1152,256]{1,0:T(8,128)(2,1)}, bf...) custom-call(s32[1]{0:T(128)} %bitcast.1.z_ref, ...), custom_call_target="tpu_custom_call" | custom-call | flops 3019898880 | bytes 9437184 | tf_op jit(solution)/shard_map/near_blocks/pallas_call | solution.py:323
  69.6 7.5 %rows_back.1 = bf16[256,5120]{1,0:T(8,128)(2,1)} custom-call(bf16[1152,256]{1,0:T(8,128)(2,1)} %get-tuple-element.49.after.own_a, bf16[320,768]{1,0:T(8,128)(2,1)S(1)} %get-tuple-element.50.act_ref, bf16[320,768]{1,0:T(8,128)(2,1)S(1)} %get-tuple-element.47.gg_ref, bf16[320,768]{1,0:T(8,128)(2,1)S(1)} %get-tuple-element.48.gu_ref, ...), custom_call_target="tpu_custom_call" | custom-call | flops 3019898880 | bytes 9437184 | tf_op jit(solution)/shard_map/rows_back/pallas_call | solution.py:474
  77.1 6.2 %all-to-all-start.1 = ((bf16[32,8,5120]{2,1,0:T(8,128)(2,1)}), bf16[32,8,5120]{2,1,0:T(8,128)(2,1)S(1)}, u32[]{:S(2)}, u32[]{:S(2)}) async-start(bf16[32,8,5120]{2,1,0:T(8,128)(2,1)} %bitcast.21), calls=%async_computation.1 | async-start | bytes 5242880 | tf_op jit(solution)/shard_map/all_to_all | solution.py:552
  83.3 0.0 collective-permute-done.r_any
  83.3 0.0 collective-permute-done.1.l_any
  83.3 2.6 %ring_step.5 = (bf16[1152,256]{1,0:T(8,128)(2,1)}, bf16[1152,256]{1,0:T(8,128)(2,1)}) custom-call(bf16[1152,256]{1,0:T(8,128)(2,1)} %get-tuple-element.49.after.own_a, bf16[1152,256]{1,0:T(8,128)(2,1)} %get-tuple-element.54.own_r, bf16[1152,256]{1,0:T(8,128)(2,1)} %get-tuple-element.55.own_l, bf16[1152,256]{1,0:T(8,128)(2,1)} %collective-permute-done.r_any, ...), custom_call_target="tpu_custom_call" | custom-call | flops 10000000000 | tf_op jit(solution)/shard_map/ring_step/pallas_call | solution.py:513
  85.9 0.8 collective-permute-start.5
  86.7 1.3 collective-permute-start.4
  88.0 0.0 collective-permute-done.2.r_any
  88.0 0.0 collective-permute-done.3.l_any
  88.0 2.5 %ring_step.6 = (bf16[1152,256]{1,0:T(8,128)(2,1)}, bf16[1152,256]{1,0:T(8,128)(2,1)}) custom-call(bf16[1152,256]{1,0:T(8,128)(2,1)} %get-tuple-element.58.after, bf16[1152,256]{1,0:T(8,128)(2,1)} %get-tuple-element.59.own_r, bf16[1152,256]{1,0:T(8,128)(2,1)} %get-tuple-element.60.own_l, bf16[1152,256]{1,0:T(8,128)(2,1)S(1)} %collective-permute-done.2.r_any, ...), custom_call_target="tpu_custom_call" | custom-call | flops 10000000000 | tf_op jit(solution)/shard_map/ring_step/pallas_call | solution.py:513
  90.5 2.0 %collective-permute-start.7 = (bf16[1152,256]{1,0:T(8,128)(2,1)}, bf16[1152,256]{1,0:T(8,128)(2,1)S(1)}, u32[]{:S(2)}, u32[]{:S(2)}) collective-permute-start(bf16[1152,256]{1,0:T(8,128)(2,1)} %get-tuple-element.70), channel_id=1, source_target_pairs={{0,224},{32,0},{64,32},{96,64},{128,96},{160,128},{192,160},{224,1... | collective-permute-start | bytes 1769480 | tf_op jit(solution)/shard_map/ppermute | solution.py:529
  92.5 0.1 collective-permute-start.6
  92.6 9.8 %collective-permute-done.5.l_any = bf16[1152,256]{1,0:T(8,128)(2,1)S(1)} collective-permute-done((bf16[1152,256]{1,0:T(8,128)(2,1)}, bf16[1152,256]{1,0:T(8,128)(2,1)S(1)}, u32[]{:S(2)}, u32[]{:S(2)}) %collective-permute-start.5) | collective-permute-done | bytes 589856 | tf_op jit(solution)/shard_map/ppermute | solution.py:529
  102.4 2.0 %collective-permute-done.4.r_any = bf16[1152,256]{1,0:T(8,128)(2,1)S(1)} collective-permute-done((bf16[1152,256]{1,0:T(8,128)(2,1)}, bf16[1152,256]{1,0:T(8,128)(2,1)S(1)}, u32[]{:S(2)}, u32[]{:S(2)}) %collective-permute-start.4) | collective-permute-done | bytes 589856 | tf_op jit(solution)/shard_map/ppermute | solution.py:529
  104.3 2.3 %ring_step.7 = (bf16[1152,256]{1,0:T(8,128)(2,1)}, bf16[1152,256]{1,0:T(8,128)(2,1)}) custom-call(bf16[1152,256]{1,0:T(8,128)(2,1)} %get-tuple-element.63.after, bf16[1152,256]{1,0:T(8,128)(2,1)} %get-tuple-element.64.own_r, bf16[1152,256]{1,0:T(8,128)(2,1)} %get-tuple-element.65.own_l, bf16[1152,256]{1,0:T(8,128)(2,1)S(1)} %collective-permute-done.4.r_any, ...), custom_call_target="tpu_custom_call" | custom-call | flops 10000000000 | tf_op jit(solution)/shard_map/ring_step/pallas_call | solution.py:513
  106.6 0.1 collective-permute-start.11
  106.7 2.0 %collective-permute-start.10 = (bf16[1152,256]{1,0:T(8,128)(2,1)}, bf16[1152,256]{1,0:T(8,128)(2,1)S(1)}, u32[]{:S(2)}, u32[]{:S(2)}) collective-permute-start(bf16[1152,256]{1,0:T(8,128)(2,1)} %get-tuple-element.67.after), channel_id=1, source_target_pairs={{0,32},{32,64},{64,96},{96,128},{128,160},{160,192},{192,224},{224... | collective-permute-start | bytes 1769480 | tf_op jit(solution)/shard_map/ppermute | solution.py:529
  108.7 6.3 %collective-permute-done.7.l_any = bf16[1152,256]{1,0:T(8,128)(2,1)S(1)} collective-permute-done((bf16[1152,256]{1,0:T(8,128)(2,1)}, bf16[1152,256]{1,0:T(8,128)(2,1)S(1)}, u32[]{:S(2)}, u32[]{:S(2)}) %collective-permute-start.7) | collective-permute-done | bytes 589856 | tf_op jit(solution)/shard_map/ppermute | solution.py:529
  115.0 2.0 %collective-permute-done.6.r_any = bf16[1152,256]{1,0:T(8,128)(2,1)S(1)} collective-permute-done((bf16[1152,256]{1,0:T(8,128)(2,1)}, bf16[1152,256]{1,0:T(8,128)(2,1)S(1)}, u32[]{:S(2)}, u32[]{:S(2)}) %collective-permute-start.6) | collective-permute-done | bytes 589856 | tf_op jit(solution)/shard_map/ppermute | solution.py:529
  117.0 2.3 %ring_step.8 = (bf16[1152,256]{1,0:T(8,128)(2,1)}, bf16[1152,256]{1,0:T(8,128)(2,1)}) custom-call(bf16[1152,256]{1,0:T(8,128)(2,1)} %get-tuple-element.67.after, bf16[1152,256]{1,0:T(8,128)(2,1)} %get-tuple-element.68.own_r, bf16[1152,256]{1,0:T(8,128)(2,1)} %get-tuple-element.69.own_l, bf16[1152,256]{1,0:T(8,128)(2,1)S(1)} %collective-permute-done.6.r_any, ...), custom_call_target="tpu_custom_call" | custom-call | flops 10000000000 | tf_op jit(solution)/shard_map/ring_step/pallas_call | solution.py:513
  119.3 0.1 collective-permute-start.8
  119.4 2.0 %collective-permute-start.9 = (bf16[1152,256]{1,0:T(8,128)(2,1)}, bf16[1152,256]{1,0:T(8,128)(2,1)S(1)}, u32[]{:S(2)}, u32[]{:S(2)}) collective-permute-start(bf16[1152,256]{1,0:T(8,128)(2,1)} %get-tuple-element.72.after), channel_id=1, source_target_pairs={{0,32},{32,64},{64,96},{96,128},{128,160},{160,192},{192,224},{224... | collective-permute-start | bytes 1769480 | tf_op jit(solution)/shard_map/ppermute | solution.py:529
  121.4 6.3 %collective-permute-done.11.l_any = bf16[1152,256]{1,0:T(8,128)(2,1)S(1)} collective-permute-done((bf16[1152,256]{1,0:T(8,128)(2,1)}, bf16[1152,256]{1,0:T(8,128)(2,1)S(1)}, u32[]{:S(2)}, u32[]{:S(2)}) %collective-permute-start.11) | collective-permute-done | bytes 589856 | tf_op jit(solution)/shard_map/ppermute | solution.py:529
  127.7 2.0 %collective-permute-done.10.r_any = bf16[1152,256]{1,0:T(8,128)(2,1)S(1)} collective-permute-done((bf16[1152,256]{1,0:T(8,128)(2,1)}, bf16[1152,256]{1,0:T(8,128)(2,1)S(1)}, u32[]{:S(2)}, u32[]{:S(2)}) %collective-permute-start.10) | collective-permute-done | bytes 589856 | tf_op jit(solution)/shard_map/ppermute | solution.py:529
  129.6 0.0 copy-start.4
  129.6 2.3 %ring_step.9 = (bf16[1152,256]{1,0:T(8,128)(2,1)}, bf16[1152,256]{1,0:T(8,128)(2,1)}) custom-call(bf16[1152,256]{1,0:T(8,128)(2,1)} %get-tuple-element.72.after, bf16[1152,256]{1,0:T(8,128)(2,1)} %get-tuple-element.75.own_r, bf16[1152,256]{1,0:T(8,128)(2,1)} %get-tuple-element.76.own_l, bf16[1152,256]{1,0:T(8,128)(2,1)S(1)} %collective-permute-done.10.r_any, ...), custom_call_target="tpu_custom_call" | custom-call | flops 10000000000 | tf_op jit(solution)/shard_map/ring_step/pallas_call | solution.py:513
  131.9 0.2 collective-permute-start.12
  132.1 3.1 %collective-permute-start.13 = (bf16[1152,256]{1,0:T(8,128)(2,1)}, bf16[1152,256]{1,0:T(8,128)(2,1)}, u32[]{:S(2)}, u32[]{:S(2)}) collective-permute-start(bf16[1152,256]{1,0:T(8,128)(2,1)} %get-tuple-element.79), channel_id=1, source_target_pairs={{0,224},{32,0},{64,32},{96,64},{128,96},{160,128},{192,160},{224,1... | collective-permute-start | bytes 1769480 | tf_op jit(solution)/shard_map/ppermute | solution.py:529
  135.3 5.1 %collective-permute-done.8.al_any = bf16[1152,256]{1,0:T(8,128)(2,1)S(1)} collective-permute-done((bf16[1152,256]{1,0:T(8,128)(2,1)}, bf16[1152,256]{1,0:T(8,128)(2,1)S(1)}, u32[]{:S(2)}, u32[]{:S(2)}) %collective-permute-start.8) | collective-permute-done | bytes 589856 | tf_op jit(solution)/shard_map/ppermute | solution.py:529
  140.3 2.0 %collective-permute-done.9.br_any = bf16[1152,256]{1,0:T(8,128)(2,1)S(1)} collective-permute-done((bf16[1152,256]{1,0:T(8,128)(2,1)}, bf16[1152,256]{1,0:T(8,128)(2,1)S(1)}, u32[]{:S(2)}, u32[]{:S(2)}) %collective-permute-start.9) | collective-permute-done | bytes 589856 | tf_op jit(solution)/shard_map/ppermute | solution.py:529
  142.3 1.5 almost.1
  143.8 0.0 copy-start
  143.8 1.0 copy-done
  144.8 0.0 copy-start.2
  144.8 1.0 copy-done.2
  145.9 0.0 all-to-all-done.1
  145.9 0.0 copy-start.1
  145.9 0.0 copy-start.3
  145.9 0.0 copy-done.4
  145.9 2.0 %unpack.1 = (bf16[160,2048]{1,0:T(8,128)(2,1)}, bf16[160,2048]{1,0:T(8,128)(2,1)}) custom-call(s32[1,160]{1,0:T(1,128)S(1)} %bitcast.14, bf16[256,5120]{1,0:T(8,128)(2,1)S(1)} %bitcast.12), custom_call_target="tpu_custom_call" | custom-call | tf_op jit(solution)/shard_map/unpack/pallas_call | solution.py:160
  147.8 6.0 %collective-permute-done.12.ar_any = bf16[1152,256]{1,0:T(8,128)(2,1)S(1)} collective-permute-done((bf16[1152,256]{1,0:T(8,128)(2,1)}, bf16[1152,256]{1,0:T(8,128)(2,1)S(1)}, u32[]{:S(2)}, u32[]{:S(2)}) %collective-permute-start.12) | collective-permute-done | bytes 589856 | tf_op jit(solution)/shard_map/ppermute | solution.py:529
  153.8 0.0 collective-permute-done.13.bl_any
  153.8 0.0 copy-done.1
  153.8 0.0 copy-done.3
  153.8 2.3 %finish.1 = (bf16[96,2048]{1,0:T(8,128)(2,1)}, bf16[256,768]{1,0:T(8,128)(2,1)}, bf16[256,768]{1,0:T(8,128)(2,1)}) custom-call(bf16[160,2048]{1,0:T(8,128)(2,1)} %get-tuple-element.39.after, f32[1152,256]{1,0:T(8,128)S(1)} %copy-done.1, f32[1152,256]{1,0:T(8,128)S(1)} %copy-done.3, bf16[1152,256]{1,0:T(8,128)(2,1)S(1)} %collective-permute-done.12.ar_any, ...), custom_call_target="tpu_custom_call" | custom-call | tf_op jit(solution)/shard_map/finish/pallas_call | solution.py:405
Async XLA Ops:
  4.2 41.6 %all-to-all-start = ((bf16[32,8,5120]{2,1,0:T(8,128)(2,1)}), bf16[32,8,5120]{2,1,0:T(8,128)(2,1)}, u32[]{:S(2)}, u32[]{:S(2)}) async-start(bf16[32,8,5120]{2,1,0:T(8,128)(2,1)} %bitcast.22), calls=%async_computation | async-start | bytes 5242880 | tf_op jit(solution)/shard_map/all_to_all | solution.py:552
  55.3 28.0 %collective-permute-start = (bf16[1152,256]{1,0:T(8,128)(2,1)}, bf16[1152,256]{1,0:T(8,128)(2,1)}, u32[]{:S(2)}, u32[]{:S(2)}) collective-permute-start(bf16[1152,256]{1,0:T(8,128)(2,1)} %get-tuple-element.56), channel_id=1, source_target_pairs={{0,32},{32,64},{64,96},{96,128},{128,160},{160,192},{192,224},{224... | collective-permute-start | bytes 1769480 | tf_op jit(solution)/shard_map/ppermute | solution.py:529
  57.3 26.0 %collective-permute-start.1 = (bf16[1152,256]{1,0:T(8,128)(2,1)}, bf16[1152,256]{1,0:T(8,128)(2,1)}, u32[]{:S(2)}, u32[]{:S(2)}) collective-permute-start(bf16[1152,256]{1,0:T(8,128)(2,1)} %get-tuple-element.57), channel_id=1, source_target_pairs={{0,224},{32,0},{64,32},{96,64},{128,96},{160,128},{192,160},{224,1... | collective-permute-start | bytes 1769480 | tf_op jit(solution)/shard_map/ppermute | solution.py:529
  61.3 26.7 %collective-permute-start.2 = (bf16[1152,256]{1,0:T(8,128)(2,1)}, bf16[1152,256]{1,0:T(8,128)(2,1)S(1)}, u32[]{:S(2)}, u32[]{:S(2)}) collective-permute-start(bf16[1152,256]{1,0:T(8,128)(2,1)} %get-tuple-element.61), channel_id=1, source_target_pairs={{0,32},{32,64},{64,96},{96,128},{128,160},{160,192},{192,224},{224... | collective-permute-start | bytes 1769480 | tf_op jit(solution)/shard_map/ppermute | solution.py:529
  61.3 26.7 %collective-permute-start.3 = (bf16[1152,256]{1,0:T(8,128)(2,1)}, bf16[1152,256]{1,0:T(8,128)(2,1)}, u32[]{:S(2)}, u32[]{:S(2)}) collective-permute-start(bf16[1152,256]{1,0:T(8,128)(2,1)} %get-tuple-element.62), channel_id=1, source_target_pairs={{0,224},{32,0},{64,32},{96,64},{128,96},{160,128},{192,160},{224,1... | collective-permute-start | bytes 1769480 | tf_op jit(solution)/shard_map/ppermute | solution.py:529
  77.1 68.7 %all-to-all-start.1 = ((bf16[32,8,5120]{2,1,0:T(8,128)(2,1)}), bf16[32,8,5120]{2,1,0:T(8,128)(2,1)S(1)}, u32[]{:S(2)}, u32[]{:S(2)}) async-start(bf16[32,8,5120]{2,1,0:T(8,128)(2,1)} %bitcast.21), calls=%async_computation.1 | async-start | bytes 5242880 | tf_op jit(solution)/shard_map/all_to_all | solution.py:552
  85.9 16.5 %collective-permute-start.5 = (bf16[1152,256]{1,0:T(8,128)(2,1)}, bf16[1152,256]{1,0:T(8,128)(2,1)S(1)}, u32[]{:S(2)}, u32[]{:S(2)}) collective-permute-start(bf16[1152,256]{1,0:T(8,128)(2,1)} %get-tuple-element.66), channel_id=1, source_target_pairs={{0,224},{32,0},{64,32},{96,64},{128,96},{160,128},{192,160},{224,1... | collective-permute-start | bytes 1769480 | tf_op jit(solution)/shard_map/ppermute | solution.py:529
  86.7 17.6 %collective-permute-start.4 = (bf16[1152,256]{1,0:T(8,128)(2,1)}, bf16[1152,256]{1,0:T(8,128)(2,1)S(1)}, u32[]{:S(2)}, u32[]{:S(2)}) collective-permute-start(bf16[1152,256]{1,0:T(8,128)(2,1)} %get-tuple-element.58.after), channel_id=1, source_target_pairs={{0,32},{32,64},{64,96},{96,128},{128,160},{160,192},{192,224},{224... | collective-permute-start | bytes 1769480 | tf_op jit(solution)/shard_map/ppermute | solution.py:529
  90.5 24.5 %collective-permute-start.7 = (bf16[1152,256]{1,0:T(8,128)(2,1)}, bf16[1152,256]{1,0:T(8,128)(2,1)S(1)}, u32[]{:S(2)}, u32[]{:S(2)}) collective-permute-start(bf16[1152,256]{1,0:T(8,128)(2,1)} %get-tuple-element.70), channel_id=1, source_target_pairs={{0,224},{32,0},{64,32},{96,64},{128,96},{160,128},{192,160},{224,1... | collective-permute-start | bytes 1769480 | tf_op jit(solution)/shard_map/ppermute | solution.py:529
  92.5 24.5 %collective-permute-start.6 = (bf16[1152,256]{1,0:T(8,128)(2,1)}, bf16[1152,256]{1,0:T(8,128)(2,1)S(1)}, u32[]{:S(2)}, u32[]{:S(2)}) collective-permute-start(bf16[1152,256]{1,0:T(8,128)(2,1)} %get-tuple-element.63.after), channel_id=1, source_target_pairs={{0,32},{32,64},{64,96},{96,128},{128,160},{160,192},{192,224},{224... | collective-permute-start | bytes 1769480 | tf_op jit(solution)/shard_map/ppermute | solution.py:529
  106.6 21.0 %collective-permute-start.11 = (bf16[1152,256]{1,0:T(8,128)(2,1)}, bf16[1152,256]{1,0:T(8,128)(2,1)S(1)}, u32[]{:S(2)}, u32[]{:S(2)}) collective-permute-start(bf16[1152,256]{1,0:T(8,128)(2,1)} %get-tuple-element.77), channel_id=1, source_target_pairs={{0,224},{32,0},{64,32},{96,64},{128,96},{160,128},{192,160},{224,1... | collective-permute-start | bytes 1769480 | tf_op jit(solution)/shard_map/ppermute | solution.py:529
  106.7 22.9 %collective-permute-start.10 = (bf16[1152,256]{1,0:T(8,128)(2,1)}, bf16[1152,256]{1,0:T(8,128)(2,1)S(1)}, u32[]{:S(2)}, u32[]{:S(2)}) collective-permute-start(bf16[1152,256]{1,0:T(8,128)(2,1)} %get-tuple-element.67.after), channel_id=1, source_target_pairs={{0,32},{32,64},{64,96},{96,128},{128,160},{160,192},{192,224},{224... | collective-permute-start | bytes 1769480 | tf_op jit(solution)/shard_map/ppermute | solution.py:529
  119.3 21.0 %collective-permute-start.8 = (bf16[1152,256]{1,0:T(8,128)(2,1)}, bf16[1152,256]{1,0:T(8,128)(2,1)S(1)}, u32[]{:S(2)}, u32[]{:S(2)}) collective-permute-start(bf16[1152,256]{1,0:T(8,128)(2,1)} %get-tuple-element.71), channel_id=1, source_target_pairs={{0,224},{32,0},{64,32},{96,64},{128,96},{160,128},{192,160},{224,1... | collective-permute-start | bytes 1769480 | tf_op jit(solution)/shard_map/ppermute | solution.py:529
  119.4 22.9 %collective-permute-start.9 = (bf16[1152,256]{1,0:T(8,128)(2,1)}, bf16[1152,256]{1,0:T(8,128)(2,1)S(1)}, u32[]{:S(2)}, u32[]{:S(2)}) collective-permute-start(bf16[1152,256]{1,0:T(8,128)(2,1)} %get-tuple-element.72.after), channel_id=1, source_target_pairs={{0,32},{32,64},{64,96},{96,128},{128,160},{160,192},{192,224},{224... | collective-permute-start | bytes 1769480 | tf_op jit(solution)/shard_map/ppermute | solution.py:529
  129.6 16.2 %copy-start.4 = (s32[160,1]{0,1:T(1,128)S(1)}, s32[160,1]{0,1:T(1,128)}, u32[]{:S(2)}) copy-start(s32[160,1]{0,1:T(1,128)} %param.7) | copy-start | bytes 1924
  131.9 21.9 %collective-permute-start.12 = (bf16[1152,256]{1,0:T(8,128)(2,1)}, bf16[1152,256]{1,0:T(8,128)(2,1)S(1)}, u32[]{:S(2)}, u32[]{:S(2)}) collective-permute-start(bf16[1152,256]{1,0:T(8,128)(2,1)} %get-tuple-element.78), channel_id=1, source_target_pairs={{0,32},{32,64},{64,96},{96,128},{128,160},{160,192},{192,224},{224... | collective-permute-start | bytes 1769480 | tf_op jit(solution)/shard_map/ppermute | solution.py:529
  132.1 21.7 %collective-permute-start.13 = (bf16[1152,256]{1,0:T(8,128)(2,1)}, bf16[1152,256]{1,0:T(8,128)(2,1)}, u32[]{:S(2)}, u32[]{:S(2)}) collective-permute-start(bf16[1152,256]{1,0:T(8,128)(2,1)} %get-tuple-element.79), channel_id=1, source_target_pairs={{0,224},{32,0},{64,32},{96,64},{128,96},{160,128},{192,160},{224,1... | collective-permute-start | bytes 1769480 | tf_op jit(solution)/shard_map/ppermute | solution.py:529
  143.8 1.0 copy-start
  144.8 1.0 copy-start.2
  145.9 7.9 %copy-start.1 = (f32[1152,256]{1,0:T(8,128)S(1)}, f32[1152,256]{1,0:T(8,128)}, u32[]{:S(2)}) copy-start(f32[1152,256]{1,0:T(8,128)} %copy-done) | copy-start | bytes 3538948
  145.9 7.9 %copy-start.3 = (f32[1152,256]{1,0:T(8,128)S(1)}, f32[1152,256]{1,0:T(8,128)}, u32[]{:S(2)}) copy-start(f32[1152,256]{1,0:T(8,128)} %copy-done.2) | copy-start | bytes 3538948
